TPU v7x, 32 devices: a whole 2x2x4 slice. The times are simulated.
32 devices in a mesh: shard: 2 (over x), ctx: 4 (over y, core), tp: 4 (over z).
Axes of the slice: x: 2, y: 2, z: 4, core: 2. Of those that a mesh axis runs over, the one named last changes fastest.
Arguments:
- inputs: bfloat16 [4, 1536, 768], P('shard', 'ctx'), may hold values from -6 to 6
- cotangent: bfloat16 [4, 1536, 768], P('shard', 'ctx'), may hold values from -6 to 6
- ln1_gain: float32 [768], replicated, may hold values from 0.25 to 1.75
- ln1_bias: float32 [768], replicated, may hold values from -4 to 4
- w_qkv: bfloat16 [3, 768, 768], P(None, 'shard', 'tp'), may hold values from -0.21875 to 0.21875
- q_bias: float32 [768], P('tp'), may hold values from -6 to 6
- v_bias: float32 [768], P('tp'), may hold values from -1.5 to 1.5
- w_out: bfloat16 [768, 768], P('tp', 'shard'), may hold values from -2.5 to 2.5
- out_bias: float32 [768], replicated, may hold values from -4 to 4
- ln2_gain: float32 [768], replicated, may hold values from 0.25 to 1.75
- ln2_bias: float32 [768], replicated, may hold values from -4 to 4
- w_up: bfloat16 [768, 3072], P('shard', 'tp'), may hold values from -0.21875 to 0.21875
- up_bias: float32 [3072], P('tp'), may hold values from -6 to 6
- w_down: bfloat16 [3072, 768], P('tp', 'shard'), may hold values from -0.109375 to 0.109375
- down_bias: float32 [768], replicated, may hold values from -4 to 4
Outputs:
- output: bfloat16 [4, 1536, 768], P('shard', 'ctx')
- grad_inputs: bfloat16 [4, 1536, 768], P('shard', 'ctx')
- grad_ln1_gain: float32 [768], replicated
- grad_ln1_bias: float32 [768], replicated
- grad_qkv: float32 [3, 768, 768], P(None, 'shard', 'tp')
- grad_q_bias: float32 [768], P('tp')
- grad_v_bias: float32 [768], P('tp')
- grad_w_out: float32 [768, 768], P('tp', 'shard')
- grad_out_bias: float32 [768], replicated
- grad_ln2_gain: float32 [768], replicated
- grad_ln2_bias: float32 [768], replicated
- grad_w_up: float32 [768, 3072], P('shard', 'tp')
- grad_up_bias: float32 [3072], P('tp')
- grad_w_down: float32 [3072, 768], P('tp', 'shard')
- grad_down_bias: float32 [768], replicated
All inputs are finite; a program needn't handle non-finite values.
Results may differ from a plain program's by a relative error of at most 0.02.
Values may be sent and summed in bfloat16 or wider, within the bound.
A program may use at most 128 MiB of HBM per device.

v0:
```python
import jax
import jax.numpy as jnp
from jax import lax
from jax.sharding import PartitionSpec as P

HEAD_DIM = 64


norm_eps = 1e-05
inv_root_two = 0.7071067811865476
inv_root_tau = 0.3989422804014327


def norm_rows(inputs_f, gain_vec, bias_vec):
    row_mean = jnp.mean(inputs_f, -1, keepdims=True)
    centred = inputs_f - row_mean
    row_var = jnp.mean(centred * centred, -1, keepdims=True)
    inv_std = lax.rsqrt(row_var + norm_eps)
    unit_rows = centred * inv_std
    return (unit_rows * gain_vec + bias_vec, unit_rows, inv_std)


def norm_back(upstream, unit_rows, inv_std, gain_vec):
    scaled = upstream * gain_vec
    inner = (
        scaled
        - jnp.mean(scaled, -1, keepdims=True)
        - unit_rows * jnp.mean(scaled * unit_rows, -1, keepdims=True)
    )
    return inv_std * inner


def gelu_slope(pre_act):
    cumulative = 0.5 * (1.0 + lax.erf(pre_act * inv_root_two))
    density = jnp.exp(-0.5 * pre_act * pre_act) * inv_root_tau
    return cumulative + pre_act * density


def tp_total(values):
    return lax.psum(values.astype(jnp.bfloat16), "tp").astype(jnp.float32)


def shards(
    inputs,
    cotangent,
    ln1_gain,
    ln1_bias,
    w_qkv,
    q_bias,
    v_bias,
    w_out,
    out_bias,
    ln2_gain,
    ln2_bias,
    w_up,
    up_bias,
    w_down,
    down_bias,
):
    clip_count, block_len, model_width = inputs.shape
    count_of_rows = clip_count * block_len
    share_rows = count_of_rows // lax.axis_size("tp")
    share_start = lax.axis_index("tp") * share_rows

    def rows_part(values):
        return lax.dynamic_slice_in_dim(values, share_start, share_rows, 0)

    wqkv_full, wout_full, wup_full, wdown_full = (
        lax.all_gather(w_qkv, "shard", axis=1, tiled=True),
        lax.all_gather(w_out, "shard", axis=1, tiled=True),
        lax.all_gather(w_up, "shard", axis=0, tiled=True),
        lax.all_gather(w_down, "shard", axis=1, tiled=True),
    )
    shard_local_width = wqkv_full.shape[2]
    heads_local = shard_local_width // HEAD_DIM
    attn_scale = HEAD_DIM ** (-0.5)
    x_rows = inputs.astype(jnp.float32).reshape(count_of_rows, model_width)
    normed_one, unit_one, inv_one = norm_rows(x_rows, ln1_gain, ln1_bias)
    act_one = normed_one.astype(jnp.bfloat16)
    projected = jnp.einsum("rd,kdc->krc", act_one, wqkv_full, preferred_element_type=jnp.float32)
    queries = (projected[0] + q_bias).astype(jnp.bfloat16)
    key_rows = projected[1].astype(jnp.bfloat16)
    value_rows = (projected[2] + v_bias).astype(jnp.bfloat16)
    q_heads = queries.reshape(clip_count, block_len, heads_local, HEAD_DIM)
    key_blocks = key_rows.reshape(clip_count, block_len, shard_local_width)
    value_blocks = value_rows.reshape(clip_count, block_len, shard_local_width)
    run_max = jnp.full((clip_count, heads_local, block_len), -1e30, jnp.float32)
    key_piece = lax.all_gather(key_blocks, "ctx", axis=1, tiled=True)
    value_piece = lax.all_gather(value_blocks, "ctx", axis=1, tiled=True)
    piece_len = key_piece.shape[1]
    key_heads = key_piece.reshape(clip_count, piece_len, heads_local, HEAD_DIM)
    value_heads = value_piece.reshape(clip_count, piece_len, heads_local, HEAD_DIM)
    scores = (
        jnp.einsum("cqhe,cnhe->chqn", q_heads, key_heads, preferred_element_type=jnp.float32)
        * attn_scale
    )
    new_max = jnp.maximum(run_max, jnp.max(scores, -1))
    expo = jnp.exp(scores - new_max[..., None])
    run_sum = jnp.sum(expo, -1)
    weighted = jnp.einsum(
        "chqn,cnhe->chqe",
        expo.astype(jnp.bfloat16),
        value_heads,
        preferred_element_type=jnp.float32,
    )
    run_max, run_sum, weighted = (new_max, run_sum, weighted)
    log_norm = run_max + jnp.log(run_sum)
    attn_heads = jnp.transpose(weighted / run_sum[..., None], (0, 2, 1, 3))
    attn_rows = attn_heads.reshape(count_of_rows, shard_local_width)
    attn_low = attn_rows.astype(jnp.bfloat16)
    attn_term = jnp.dot(attn_low, wout_full, preferred_element_type=jnp.float32)
    residual = x_rows + tp_total(attn_term) + out_bias
    normed_two, unit_two, inv_two = norm_rows(residual, ln2_gain, ln2_bias)
    act_two = normed_two.astype(jnp.bfloat16)
    hidden_pre = jnp.dot(act_two, wup_full, preferred_element_type=jnp.float32) + up_bias
    hidden = jax.nn.gelu(hidden_pre, approximate=False).astype(jnp.bfloat16)
    branch_term = jnp.dot(hidden, wdown_full, preferred_element_type=jnp.float32)
    output = (
        (residual + tp_total(branch_term) + down_bias)
        .astype(jnp.bfloat16)
        .reshape(clip_count, block_len, model_width)
    )
    wqkv_full, wout_full, wup_full, wdown_full = (
        lax.all_gather(w_qkv, "shard", axis=1, tiled=True),
        lax.all_gather(w_out, "shard", axis=1, tiled=True),
        lax.all_gather(w_up, "shard", axis=0, tiled=True),
        lax.all_gather(w_down, "shard", axis=1, tiled=True),
    )
    grad_y = cotangent.astype(jnp.float32).reshape(count_of_rows, model_width)
    grad_db = jnp.sum(rows_part(grad_y), 0)
    grad_ylow = grad_y.astype(jnp.bfloat16)
    grad_wdown = jnp.einsum("rf,rd->fd", hidden, grad_ylow, preferred_element_type=jnp.float32)
    grad_hidden = jnp.einsum("rd,fd->rf", grad_ylow, wdown_full, preferred_element_type=jnp.float32)
    grad_pre = (grad_hidden * gelu_slope(hidden_pre)).astype(jnp.bfloat16)
    grad_ub = jnp.sum(grad_pre.astype(jnp.float32), 0)
    grad_wup = jnp.einsum("rd,rf->df", act_two, grad_pre, preferred_element_type=jnp.float32)
    acttwo_term = jnp.einsum("rf,df->rd", grad_pre, wup_full, preferred_element_type=jnp.float32)
    grad_acttwo = tp_total(acttwo_term)
    grad_resid = grad_y + norm_back(grad_acttwo, unit_two, inv_two, ln2_gain)
    grad_g2 = jnp.sum(rows_part(grad_acttwo) * rows_part(unit_two), 0)
    grad_b2 = jnp.sum(rows_part(grad_acttwo), 0)
    grad_ob = jnp.sum(rows_part(grad_resid), 0)
    grad_mixed = grad_resid.astype(jnp.bfloat16)
    grad_wout = jnp.einsum("rc,rd->cd", attn_low, grad_mixed, preferred_element_type=jnp.float32)
    grad_attn = jnp.einsum(
        "rd,cd->rc", grad_mixed, wout_full, preferred_element_type=jnp.float32
    ).astype(jnp.bfloat16)
    grad_heads = grad_attn.reshape(clip_count, block_len, heads_local, HEAD_DIM)
    row_dots = jnp.transpose(jnp.sum(grad_heads.astype(jnp.float32) * attn_heads, -1), (0, 2, 1))
    key_piece = lax.all_gather(key_blocks, "ctx", axis=1, tiled=True)
    value_piece = lax.all_gather(value_blocks, "ctx", axis=1, tiled=True)
    piece_len = key_piece.shape[1]
    key_heads = key_piece.reshape(clip_count, piece_len, heads_local, HEAD_DIM)
    value_heads = value_piece.reshape(clip_count, piece_len, heads_local, HEAD_DIM)
    scores = (
        jnp.einsum("cqhe,cnhe->chqn", q_heads, key_heads, preferred_element_type=jnp.float32)
        * attn_scale
    )
    probs = jnp.exp(scores - log_norm[..., None])
    grad_prob = jnp.einsum(
        "cqhe,cnhe->chqn", grad_heads, value_heads, preferred_element_type=jnp.float32
    )
    grad_score = (probs * (grad_prob - row_dots[..., None])).astype(jnp.bfloat16)
    grad_query = (
        jnp.einsum("chqn,cnhe->chqe", grad_score, key_heads, preferred_element_type=jnp.float32)
        * attn_scale
    )
    piece_key = (
        jnp.einsum("chqn,cqhe->cnhe", grad_score, q_heads, preferred_element_type=jnp.float32)
        * attn_scale
    )
    piece_value = jnp.einsum(
        "chqn,cqhe->cnhe",
        probs.astype(jnp.bfloat16),
        grad_heads,
        preferred_element_type=jnp.float32,
    )
    joined = jnp.concatenate(
        [
            piece_key.reshape(clip_count, piece_len, shard_local_width),
            piece_value.reshape(clip_count, piece_len, shard_local_width),
        ],
        -1,
    )
    grad_kv = joined
    grad_query, grad_kv = (grad_query, grad_kv)
    key_value_totals = lax.psum_scatter(
        grad_kv.astype(jnp.bfloat16), "ctx", scatter_dimension=1, tiled=True
    ).astype(jnp.float32)
    query_gradient_partial = (
        jnp.transpose(grad_query, (0, 2, 1, 3))
        .reshape(count_of_rows, shard_local_width)
        .astype(jnp.bfloat16)
    )
    key_gradient_partial = (
        key_value_totals[:, :, :shard_local_width]
        .reshape(count_of_rows, shard_local_width)
        .astype(jnp.bfloat16)
    )
    value_gradient_partial = (
        key_value_totals[:, :, shard_local_width:]
        .reshape(count_of_rows, shard_local_width)
        .astype(jnp.bfloat16)
    )
    stacked_tensors = jnp.stack(
        [query_gradient_partial, key_gradient_partial, value_gradient_partial]
    )
    grad_qb = jnp.sum(query_gradient_partial.astype(jnp.float32), 0)
    grad_vb = jnp.sum(value_gradient_partial.astype(jnp.float32), 0)
    grad_wqkv = jnp.einsum(
        "krc,rd->kdc", stacked_tensors, act_one, preferred_element_type=jnp.float32
    )
    actone_term = jnp.einsum(
        "krc,kdc->rd", stacked_tensors, wqkv_full, preferred_element_type=jnp.float32
    )
    grad_actone = tp_total(actone_term)
    input_norm = norm_back(grad_actone, unit_one, inv_one, ln1_gain)
    grad_g1 = jnp.sum(rows_part(grad_actone) * rows_part(unit_one), 0)
    grad_b1 = jnp.sum(rows_part(grad_actone), 0)
    grad_inputs = (
        (grad_resid + input_norm).astype(jnp.bfloat16).reshape(clip_count, block_len, model_width)
    )
    partial_set = (
        lax.psum_scatter(
            grad_wqkv.astype(jnp.bfloat16), "shard", scatter_dimension=1, tiled=True
        ).astype(jnp.float32),
        lax.psum_scatter(
            grad_wout.astype(jnp.bfloat16), "shard", scatter_dimension=1, tiled=True
        ).astype(jnp.float32),
        lax.psum_scatter(
            grad_wup.astype(jnp.bfloat16), "shard", scatter_dimension=0, tiled=True
        ).astype(jnp.float32),
        lax.psum_scatter(
            grad_wdown.astype(jnp.bfloat16), "shard", scatter_dimension=1, tiled=True
        ).astype(jnp.float32),
    )
    owned = (
        lax.psum(partial_set[0].astype(jnp.bfloat16), "ctx").astype(jnp.float32),
        lax.psum(partial_set[1].astype(jnp.bfloat16), "ctx").astype(jnp.float32),
        lax.psum(partial_set[2].astype(jnp.bfloat16), "ctx").astype(jnp.float32),
        lax.psum(partial_set[3].astype(jnp.bfloat16), "ctx").astype(jnp.float32),
    )
    vectors = lax.psum((grad_qb, grad_vb, grad_ub), ("shard", "ctx"))
    norm_sums = lax.psum(
        (grad_g1, grad_b1, grad_ob, grad_g2, grad_b2, grad_db), ("shard", "ctx", "tp")
    )
    return (
        output,
        grad_inputs,
        norm_sums[0],
        norm_sums[1],
        owned[0],
        vectors[0],
        vectors[1],
        owned[1],
        norm_sums[2],
        norm_sums[3],
        norm_sums[4],
        owned[2],
        vectors[2],
        owned[3],
        norm_sums[5],
    )


def solution(mesh):
    placed = (
        P("shard", "ctx", None),
        P("shard", "ctx", None),
        P(),
        P(),
        P(None, "shard", "tp"),
        P("tp"),
        P("tp"),
        P("tp", "shard"),
        P(),
        P(),
        P(),
        P("shard", "tp"),
        P("tp"),
        P("tp", "shard"),
        P(),
    )
    return jax.shard_map(
        shards,
        mesh=mesh,
        in_specs=placed,
        out_specs=(
            P("shard", "ctx", None),
            P("shard", "ctx", None),
            P(),
            P(),
            P(None, "shard", "tp"),
            P("tp"),
            P("tp"),
            P("tp", "shard"),
            P(),
            P(),
            P(),
            P("shard", "tp"),
            P("tp"),
            P("tp", "shard"),
            P(),
        ),
        check_vma=False,
    )
```

profile of v0, /device:TPU:0, one launch (start us, length us, event | category | flops | bytes accessed | tf_op | source)
XLA Modules:
  0.0 535.6 jit_solution(14505202180377104426)
XLA Ops:
  11.5 13.8 %all_gather.24 = bf16[3,768,192]{1,2,0:T(8,128)(2,1)S(1)} all-gather(bf16[3,384,192]{1,2,0:T(8,128)(2,1)S(1)} %copy-done.21), channel_id=1, replica_groups=mesh['shard'=2,'ctx'=4,'tp'=4] {'shard'}, dimensions={1}, use_global_device_ids=true | all-gather | bytes 1327104 | tf_op jit(solution)/shard_map/all_gather | solution.py:69
  32.5 5.8 %all_gather.27 = bf16[192,768]{1,0:T(8,128)(2,1)S(1)} all-gather(bf16[192,384]{1,0:T(8,128)(2,1)S(1)} %copy-done.22), channel_id=1, replica_groups=mesh['shard'=2,'ctx'=4,'tp'=4] {'shard'}, dimensions={1}, use_global_device_ids=true | all-gather | bytes 442368 | tf_op jit(solution)/shard_map/all_gather | solution.py:70
  38.3 10.2 %all-gather.5.cloned.1.call-done = bf16[2,1536,192]{1,0,2:T(2,128)(2,1)} async-done(((bf16[2,384,192]{1,0,2:T(2,128)(2,1)}), bf16[2,1536,192]{1,0,2:T(2,128)(2,1)}) %all-gather.5.cloned.1.call-update) | async-done | bytes 1179664 | tf_op jit(solution)/shard_map/all_gather | solution.py:88
  49.9 7.2 %multiply_reduce_fusion = (f32[2,3,384]{2,1,0:T(4,128)S(1)}, f32[2,3,384,1536]{3,2,1,0:T(8,128)}) fusion(bf16[2,1536,3,64]{1,3,2,0:T(8,128)(2,1)S(1)} %bitcast.108, f32[2,384,3,64]{1,0,3,2:T(2,128)S(1)} %squeeze.7, f32[3,64]{1,0:T(4,128)S(1)} %add.159), kind=kOutput, calls=%fused_computation.6 | convolution fusion | flops 460355328 | bytes 15935232 | tf_op jit(solution)/shard_map/cqhe,cnhe->chqn/dot_general | solution.py:94
  57.1 7.7 %fusion = f32[2,3,384]{2,1,0:T(4,128)S(1)} fusion(f32[2,3,384,1536]{3,2,1,0:T(8,128)} %get-tuple-element.45, f32[2,3,384]{2,1,0:T(4,128)S(1)} %broadcast_maximum_fusion), kind=kLoop, calls=%fused_computation.3 | loop fusion | flops 10614528 | bytes 14174208 | tf_op jit(solution)/shard_map/reduce_sum | solution.py:99
  69.7 8.9 %fusion.56 = (bf16[2,384,3,64]{1,3,2,0:T(8,128)(2,1)S(1)}, f32[2,384,3,64]{1,3,2,0:T(8,128)}) fusion(f32[2,384,3]{1,2,0:T(4,128)S(1)} %bitcast.137, bf16[2,1536,3,64]{1,3,2,0:T(8,128)(2,1)S(1)} %bitcast.114, f32[2,3,384,1536]{3,2,1,0:T(8,128)} %get-tuple-element.45, f32[2,3,384]{2,1,0:T(4,128)S(1)} %broadcast_maximum_fusion), kind=kOutput, calls=%fused_computation.114 | convolution fusion | flops 463896576 | bytes 16238592 | tf_op jit(solution)/shard_map/chqn,cnhe->chqe/dot_general | solution.py:100
  82.1 54.5 %all-reduce.9.cloned.1.call-done = bf16[768,768]{1,0:T(8,128)(2,1)} async-done(((bf16[768,768]{1,0:T(8,128)(2,1)}), bf16[768,768]{1,0:T(8,128)(2,1)}) %all-reduce.9.cloned.1.call-update) | async-done | bytes 1179664 | tf_op jit(solution)/shard_map/psum | solution.py:40
  140.5 8.9 %fusion.15 = (bf16[768,768]{1,0:T(8,128)(2,1)}, f32[768,768]{1,0:T(8,128)}) fusion(f32[768]{0:T(1024)S(1)} %copy-done.42, bf16[768,768]{1,0:T(8,128)(2,1)} %all-gather.9.cloned.1.call-done, f32[768,768]{1,0:T(8,128)S(1)} %subtract_multiply_fusion, f32[768]{0:T(1024)} %param.25, f32[768]{0:T(1024)S(1)} %copy-done.36), kind=kOutput, calls=%fused_computation.18 | convolution fusion | flops 946667520 | bytes 7087104 | tf_op jit(solution)/shard_map/dot_general | solution.py:115
  149.4 4.7 convert_reduce_fusion.1
  158.0 54.8 %all-reduce.11.cloned.1.call-done = bf16[768,768]{1,0:T(8,128)(2,1)} async-done(((bf16[768,768]{1,0:T(8,128)(2,1)}), bf16[768,768]{1,0:T(8,128)(2,1)}) %all-reduce.11.cloned.1.call-update) | async-done | bytes 1179664 | tf_op jit(solution)/shard_map/psum | solution.py:40
  221.6 7.9 %fusion.9 = bf16[2,3,64,1536]{3,2,1,0:T(8,128)(2,1)S(1)} fusion(f32[2,3,384,1536]{3,2,1,0:T(8,128)} %get-tuple-element.45, f32[2,3,384]{2,1,0:T(4,128)S(1)} %log_add_fusion, bf16[2,384,3,64]{1,0,3,2:T(2,128)(2,1)} %reshape.206), kind=kOutput, calls=%fused_computation.14 | convolution fusion | flops 464191488 | bytes 15639552 | tf_op jit(solution)/shard_map/chqn,cqhe->cnhe/dot_general | solution.py:172
  229.5 7.1 %multiply_convert_fusion = bf16[2,3,384,1536]{3,2,1,0:T(8,128)(2,1)S(1)} fusion(f32[2,3,384,1536]{3,2,1,0:T(8,128)} %get-tuple-element.45, bf16[2,1536,3,64]{1,3,2,0:T(8,128)(2,1)S(1)} %bitcast.115, f32[2,3,384]{2,1,0:T(4,128)S(1)} %bitcast.136, f32[2,3,384]{2,1,0:T(4,128)S(1)} %log_add_fusion, bf16[2,384,3,64]{1,0,3,2:T(2,128)(2,1)S(1)} %copy-done.12), kind=kOutput, calls=%fused_computation | convolution fusion | flops 470679552 | bytes 22726656 | tf_op jit(solution)/shard_map/cqhe,cnhe->chqn/dot_general | solution.py:160
  241.1 6.8 %copy.55 = bf16[2,1536,384]{2,0,1:T(2,128)(2,1)} copy(bf16[2,1536,384]{1,2,0:T(8,128)(2,1)} %pad_maximum_fusion) | data formatting | bytes 4718592
  255.7 4.1 convolution_convert_fusion
  262.5 5.6 %convert_reduce_fusion.3 = (f32[3,64]{1,0:T(4,128)S(1)}, bf16[2,3,384,64]{2,3,1,0:T(8,128)(2,1)S(1)}) fusion(bf16[2,3,384,1536]{3,2,1,0:T(8,128)(2,1)} %copy-done, bf16[2,1536,3,64]{1,3,2,0:T(8,128)(2,1)} %bitcast.109), kind=kOutput, calls=%fused_computation.82 | convolution fusion | flops 453574464 | bytes 8553216 | tf_op jit(solution)/shard_map/chqn,cnhe->chqe/dot_general | solution.py:165
  272.7 11.7 %reduce-scatter.16.cloned.1.call-done = bf16[384,768]{1,0:T(8,128)(2,1)} async-done(((bf16[1536,768]{1,0:T(8,128)(2,1)}), bf16[384,768]{1,0:T(8,128)(2,1)}) %reduce-scatter.16.cloned.1.call-update) | async-done | bytes 589840
  308.1 4.1 reshape.217
  312.3 4.1 convolution_convert_fusion.1
  316.5 3.9 convolution_convert_fusion.3
  336.1 14.2 %all-reduce.1 = (f32[192]{0:T(256)}, f32[192]{0:T(256)}, f32[768]{0:T(1024)}) all-reduce(f32[192]{0:T(256)} %reduce_sum.186, f32[192]{0:T(256)S(1)} %convert_reduce_fusion.2, f32[768]{0:T(1024)} %get-tuple-element.52), channel_id=1, replica_groups=mesh['shard'=2,'ctx'=4,'tp'=4] {'shard','ctx'}, use_global_device_ids=true, to_apply=%region_23.0 | all-reduce | flops 1152 | bytes 9216 | tf_op jit(solution)/shard_map/psum | solution.py:243
  354.9 16.1 %reduce-scatter.14.cloned.1.call-done = bf16[384,768]{1,0:T(8,128)(2,1)} async-done(((bf16[768,768]{1,0:T(8,128)(2,1)}), bf16[384,768]{1,0:T(8,128)(2,1)}) %reduce-scatter.14.cloned.1.call-update) | async-done | bytes 589840 | tf_op jit(solution)/shard_map/reduce_scatter | solution.py:230
  371.1 99.0 %all-reduce.13.cloned.1.call-done = (bf16[768,768]{1,0:T(8,128)(2,1)}, bf16[768,768]{1,0:T(8,128)(2,1)}) async-done(((bf16[768,768]{1,0:T(8,128)(2,1)}, bf16[768,768]{1,0:T(8,128)(2,1)}), (bf16[768,768]{1,0:T(8,128)(2,1)}, bf16[768,768]{1,0:T(8,128)(2,1)})) %all-reduce.13.cloned.1.call-update) | async-done | bytes 2359312 | tf_op jit(solution)/shard_map/psum | solution.py:40
  474.9 41.0 %all-reduce = (f32[768]{0:T(1024)}, f32[768]{0:T(1024)}, f32[768]{0:T(1024)}, f32[768]{0:T(1024)}, f32[768]{0:T(1024)}, /*index=5*/f32[768]{0:T(1024)}) all-reduce(f32[768]{0:T(1024)} %get-tuple-element.18, f32[768]{0:T(1024)} %get-tuple-element.17, ...), channel_id=1, replica_groups=mesh['shard'=2,'ctx'=4,'tp'=4] {'shard','ctx','tp'}, use_global_device_ids=true, to_apply=%region_17.0 | all-reduce | flops 4608 | bytes 36864 | tf_op jit(solution)/shard_map/psum | solution.py:244
  517.3 4.0 add_convert_fusion
  (203 shorter events, 113.2 us)
Async XLA Ops:
  8.0 17.3 %copy-start.1 = (bf16[2,384,768]{2,1,0:T(8,128)(2,1)S(1)}, bf16[2,384,768]{2,1,0:T(8,128)(2,1)}, u32[]{:S(2)}) copy-start(bf16[2,384,768]{2,1,0:T(8,128)(2,1)} %param.15) | copy-start | bytes 3538948
  8.0 40.5 %all-gather.5.cloned.1.call-start = ((), (), s32[]{:S(2)}) async-start(), calls=%async_computation.5 | async-start | bytes 1474560 | tf_op jit(solution)/shard_map/all_gather | solution.py:88
  11.5 14.3 %copy-start.25 = (f32[768]{0:T(1024)}, f32[768]{0:T(1024)S(1)}, u32[]{:S(2)}) copy-start(f32[768]{0:T(1024)S(1)} %div.38) | copy-start | bytes 9220
  11.5 14.2 %copy-start.34 = (f32[768]{0:T(1024)S(1)}, f32[768]{0:T(1024)}, u32[]{:S(2)}) copy-start(f32[768]{0:T(1024)} %param.17) | copy-start | bytes 9220
  29.3 39.0 %all-gather.7.cloned.1.call-start = ((), (), s32[]{:S(2)}) async-start(), calls=%async_computation.6 | async-start | bytes 1474560 | tf_op jit(solution)/shard_map/all_gather | solution.py:89
  32.0 104.6 %all-reduce.9.cloned.1.call-start = ((), (), s32[]{:S(2)}) async-start(), calls=%async_computation.7 | async-start | bytes 2359296 | tf_op jit(solution)/shard_map/psum | solution.py:40
  32.5 24.6 %copy-start.7 = (f32[2,384,3,64]{1,0,3,2:T(2,128)}, f32[2,384,3,64]{1,0,3,2:T(2,128)S(1)}, u32[]{:S(2)}) copy-start(f32[2,384,3,64]{1,0,3,2:T(2,128)S(1)} %squeeze.7) | copy-start | bytes 1769476
  38.3 40.7 %copy-start.15 = (bf16[192,768]{1,0:T(8,128)(2,1)}, bf16[192,768]{1,0:T(8,128)(2,1)S(1)}, u32[]{:S(2)}) copy-start(bf16[192,768]{1,0:T(8,128)(2,1)S(1)} %all_gather.27) | copy-start | bytes 884740
  78.9 57.7 %copy-start.29 = (f32[768]{0:T(1024)S(1)}, f32[768]{0:T(1024)}, u32[]{:S(2)}) copy-start(f32[768]{0:T(1024)} %param.23) | copy-start | bytes 9220
  79.0 59.5 %copy-start.14 = (bf16[24,8,2,384]{3,1,2,0:T(8,128)(2,1)}, bf16[24,8,2,384]{3,1,2,0:T(8,128)(2,1)S(1)}, u32[]{:S(2)}) copy-start(bf16[24,8,2,384]{3,1,2,0:T(8,128)(2,1)S(1)} %copy.67) | copy-start | bytes 884740
  80.6 59.7 %all-gather.9.cloned.1.call-start = ((), (), s32[]{:S(2)}) async-start(), calls=%async_computation.8 | async-start | bytes 1769472 | tf_op jit(solution)/shard_map/all_gather | solution.py:71
  81.1 68.2 %all-gather.11.cloned.1.call-start = ((), (), s32[]{:S(2)}) async-start(), calls=%async_computation.9 | async-start | bytes 1769472 | tf_op jit(solution)/shard_map/all_gather | solution.py:72
  81.7 131.1 %all-reduce.11.cloned.1.call-start = ((), (), s32[]{:S(2)}) async-start(), calls=%async_computation.10 | async-start | bytes 2359296 | tf_op jit(solution)/shard_map/psum | solution.py:40
  140.3 72.6 %copy-start.2 = (f32[768,768]{1,0:T(8,128)}, f32[768,768]{1,0:T(8,128)S(1)}, u32[]{:S(2)}) copy-start(f32[768,768]{1,0:T(8,128)S(1)} %subtract_multiply_fusion) | copy-start | bytes 7077892
  157.3 127.1 %reduce-scatter.16.cloned.1.call-start = ((), (), s32[]{:S(2)}) async-start(), calls=%async_computation.12 | async-start | bytes 2949120
  251.6 77.6 %reduce-scatter.20.cloned.1.call-start = ((), (), s32[]{:S(2)}) async-start(), calls=%async_computation.14 | async-start | bytes 589824
  255.6 75.3 %reduce-scatter.22.cloned.1.call-start = ((), (), s32[]{:S(2)}) async-start(), calls=%async_computation.15 | async-start | bytes 1769472
  262.3 88.0 %reduce-scatter.18.cloned.1.call-start = ((), (), s32[]{:S(2)}) async-start(), calls=%async_computation.13 | async-start | bytes 1474560
  312.2 58.9 %reduce-scatter.14.cloned.1.call-start = ((), (), s32[]{:S(2)}) async-start(), calls=%async_computation.11 | async-start | bytes 1769472 | tf_op jit(solution)/shard_map/reduce_scatter | solution.py:230
  316.4 153.7 %all-reduce.13.cloned.1.call-start = ((), (), s32[]{:S(2)}) async-start(), calls=%async_computation.16 | async-start | bytes 4718592 | tf_op jit(solution)/shard_map/psum | solution.py:40
  322.6 198.7 %all-reduce.15.cloned.1.call-start = ((), (), s32[]{:S(2)}) async-start(), calls=%async_computation.17 | async-start | bytes 3538944 | tf_op jit(solution)/shard_map/psum | solution.py:238
  335.0 135.1 %copy-start.26 = (f32[768]{0:T(1024)S(1)}, f32[768]{0:T(1024)}, u32[]{:S(2)}) copy-start(f32[768]{0:T(1024)} %copy-done.25) | copy-start | bytes 9220
  335.0 135.1 %copy-start.28 = (f32[768]{0:T(1024)S(1)}, f32[768]{0:T(1024)}, u32[]{:S(2)}) copy-start(f32[768]{0:T(1024)} %copy-done.27) | copy-start | bytes 9220
  473.0 44.3 %copy-start.30 = (f32[768]{0:T(1024)S(1)}, f32[768]{0:T(1024)}, u32[]{:S(2)}) copy-start(f32[768]{0:T(1024)} %param.23) | copy-start | bytes 9220
  (36 other events, 180.4 us)
Sparse Core Ops, SparseCore 0:
  29.4 19.0 all-gather.4
  50.6 17.5 all-gather.6
  80.7 55.8 all-reduce.8
  157.4 55.4 all-reduce.10
  251.7 32.5 reduce-scatter.15
  286.5 13.1 reduce-scatter.19
  301.9 21.7 reduce-scatter.21
  326.6 19.7 reduce-scatter.17
  349.3 21.7 reduce-scatter.13
  374.1 95.9 all-reduce.12
  472.9 46.8 all-reduce.14
Sparse Core Ops, SparseCore 1:
  82.6 22.6 all-gather.8
  106.6 22.7 all-gather.10
where the time goes:
time: 546 us; the launch traced here: 536 us
  waiting for transfers between devices  251 us (46%)
  matrix products  76.7 us (14%)
  blocking collectives  74.8 us (14%)
  local copies, waits for them, and re-layouts  67.2 us (12%)
  other arithmetic  48.6 us (9%)
  between operations  16.2 us (3%)
    psum x3, waiting for transfers between devices, tp_total(): return lax.psum(values.astype(jnp.bfloat16), 'tp').astype(jnp.float32)  208 us
    unnamed x109, local copies, waits for them, and re-layouts  43.8 us
    psum x1, blocking collectives, shards(): lax.psum((grad_g1, grad_b1, grad_ob, grad_g2, grad_b2, grad_db), ('shard'...  41 us
    reduce_scatter x1, waiting for transfers between devices, shards(): lax.psum_scatter(grad_wup.astype(jnp.bfloat16), 'shard', scatter_dimensio...  16.1 us
    psum x1, blocking collectives, shards(): vectors = lax.psum((grad_qb, grad_vb, grad_ub), ('shard', 'ctx'))  14.2 us
    all_gather x1, blocking collectives, shards(): lax.all_gather(w_qkv, 'shard', axis=1, tiled=True)  13.8 us
    unnamed x17, waiting for transfers between devices  12.9 us
  transfers between devices with their start and end apart: 13, of which 7 were waited for; matrix products, arithmetic and copies ran while one was open for 22% of the time, Pallas kernels for 0%

commit v1 on v0

v1 whole, which is shorter than its diff:
```python
import functools

import jax
import jax.numpy as jnp
from jax import lax
from jax.experimental import pallas as pl
from jax.experimental.pallas import tpu as pltpu
from jax.sharding import PartitionSpec as P

HEAD_DIM = 64


norm_eps = 1e-05
inv_root_two = 0.7071067811865476
inv_root_tau = 0.3989422804014327


def norm_rows(inputs_f, gain_vec, bias_vec):
    row_mean = jnp.mean(inputs_f, -1, keepdims=True)
    centred = inputs_f - row_mean
    row_var = jnp.mean(centred * centred, -1, keepdims=True)
    inv_std = lax.rsqrt(row_var + norm_eps)
    unit_rows = centred * inv_std
    return (unit_rows * gain_vec + bias_vec, unit_rows, inv_std)


def norm_back(upstream, unit_rows, inv_std, gain_vec):
    scaled = upstream * gain_vec
    inner = (
        scaled
        - jnp.mean(scaled, -1, keepdims=True)
        - unit_rows * jnp.mean(scaled * unit_rows, -1, keepdims=True)
    )
    return inv_std * inner


def gelu_slope(pre_act):
    cumulative = 0.5 * (1.0 + lax.erf(pre_act * inv_root_two))
    density = jnp.exp(-0.5 * pre_act * pre_act) * inv_root_tau
    return cumulative + pre_act * density


MESH = pl.DeviceIdType.MESH
ROW_DIMS = (((0,), (0,)), ((), ()))
LAST_DIMS = (((1,), (1,)), ((), ()))
VMEM_BYTES = 50 * 1024 * 1024


def scores_of(q_ref, kv_ref, head, width):
    cols = slice(head * HEAD_DIM, (head + 1) * HEAD_DIM)
    vcols = slice(width + head * HEAD_DIM, width + (head + 1) * HEAD_DIM)
    blocks, _, block_len, _ = kv_ref.shape
    q = q_ref[0, :, cols] * jnp.bfloat16(HEAD_DIM**-0.5)
    k = kv_ref[:, 0, :, cols].reshape(blocks * block_len, HEAD_DIM)
    v = kv_ref[:, 0, :, vcols].reshape(blocks * block_len, HEAD_DIM)
    s = lax.dot_general(k, q, LAST_DIMS, preferred_element_type=jnp.float32)
    return q, k, v, s


def attend_kernel(q_ref, kv_ref, o_ref, ot_ref, lse_ref):
    width = q_ref.shape[2]
    for head in range(width // HEAD_DIM):
        q, k, v, s = scores_of(q_ref, kv_ref, head, width)
        top = jnp.max(s, 0, keepdims=True)
        e = jnp.exp(s - top)
        total = jnp.sum(e, 0, keepdims=True)
        ot = lax.dot_general(
            v, e.astype(jnp.bfloat16), ROW_DIMS, preferred_element_type=jnp.float32
        )
        ot_ref[0, head * HEAD_DIM : (head + 1) * HEAD_DIM, :] = ot / total
        lse_ref[0, head : head + 1, :] = top + jnp.log(total)
    o_ref[0] = ot_ref[0].T.astype(jnp.bfloat16)


def attend(q, kv):
    clips, length, width = q.shape
    blocks = kv.shape[0]
    heads = width // HEAD_DIM
    work = clips * heads * length * blocks * length
    row = pl.BlockSpec((1, length, width), lambda c: (c, 0, 0))
    return pl.pallas_call(
        attend_kernel,
        grid=(clips,),
        in_specs=[row, pl.BlockSpec((blocks, 1, length, 2 * width), lambda c: (0, c, 0, 0))],
        out_specs=[
            row,
            pl.BlockSpec((1, width, length), lambda c: (c, 0, 0)),
            pl.BlockSpec((1, 8, length), lambda c: (c, 0, 0)),
        ],
        out_shape=[
            jax.ShapeDtypeStruct(q.shape, jnp.bfloat16),
            jax.ShapeDtypeStruct((clips, width, length), jnp.float32),
            jax.ShapeDtypeStruct((clips, 8, length), jnp.float32),
        ],
        compiler_params=pltpu.CompilerParams(vmem_limit_bytes=VMEM_BYTES),
        cost_estimate=pl.CostEstimate(
            flops=4 * work * HEAD_DIM, bytes_accessed=4 * q.size * 5, transcendentals=work
        ),
    )(q, kv)


def attend_back_kernel(q_ref, kv_ref, do_ref, ot_ref, lse_ref, dq_ref, dkv_ref, dqt_ref):
    width = q_ref.shape[2]
    blocks, _, block_len, _ = kv_ref.shape
    scale = HEAD_DIM**-0.5
    dot_all = do_ref[0].astype(jnp.float32).T
    for head in range(width // HEAD_DIM):
        cols = slice(head * HEAD_DIM, (head + 1) * HEAD_DIM)
        vcols = slice(width + head * HEAD_DIM, width + (head + 1) * HEAD_DIM)
        q, k, v, s = scores_of(q_ref, kv_ref, head, width)
        do = do_ref[0, :, cols]
        delta = jnp.sum(dot_all[cols, :] * ot_ref[0, cols, :], 0, keepdims=True)
        p = jnp.exp(s - lse_ref[0, head : head + 1, :])
        dp = lax.dot_general(v, do, LAST_DIMS, preferred_element_type=jnp.float32)
        ds = (p * (dp - delta)).astype(jnp.bfloat16)
        dv = jnp.dot(p.astype(jnp.bfloat16), do, preferred_element_type=jnp.float32)
        dk = jnp.dot(ds, q, preferred_element_type=jnp.float32)
        dqt_ref[cols, :] = (
            lax.dot_general(k, ds, ROW_DIMS, preferred_element_type=jnp.float32) * scale
        )
        dkv_ref[:, 0, :, cols] = dk.astype(jnp.bfloat16).reshape(blocks, block_len, HEAD_DIM)
        dkv_ref[:, 0, :, vcols] = dv.astype(jnp.bfloat16).reshape(blocks, block_len, HEAD_DIM)
    dq_ref[0] = dqt_ref[...].T.astype(jnp.bfloat16)


def attend_back(q, kv, do, ot, lse):
    clips, length, width = q.shape
    blocks = kv.shape[0]
    heads = width // HEAD_DIM
    work = clips * heads * length * blocks * length
    row = pl.BlockSpec((1, length, width), lambda c: (c, 0, 0))
    wide = pl.BlockSpec((blocks, 1, length, 2 * width), lambda c: (0, c, 0, 0))
    return pl.pallas_call(
        attend_back_kernel,
        grid=(clips,),
        in_specs=[
            row,
            wide,
            row,
            pl.BlockSpec((1, width, length), lambda c: (c, 0, 0)),
            pl.BlockSpec((1, 8, length), lambda c: (c, 0, 0)),
        ],
        out_specs=[row, wide],
        out_shape=[
            jax.ShapeDtypeStruct(q.shape, jnp.bfloat16),
            jax.ShapeDtypeStruct(kv.shape, jnp.bfloat16),
        ],
        scratch_shapes=[pltpu.VMEM((width, length), jnp.float32)],
        compiler_params=pltpu.CompilerParams(vmem_limit_bytes=VMEM_BYTES),
        cost_estimate=pl.CostEstimate(
            flops=10 * work * HEAD_DIM, bytes_accessed=4 * q.size * 10, transcendentals=work
        ),
    )(q, kv, do, ot, lse)


def greet(partners):
    barrier = pltpu.get_barrier_semaphore()
    for partner in partners:
        pl.semaphore_signal(barrier, inc=1, device_id=partner, device_id_type=MESH)
    pl.semaphore_wait(barrier, len(partners))


def remote(src, dst, sems, slot, partner):
    copy = pltpu.make_async_remote_copy(
        src_ref=src,
        dst_ref=dst,
        send_sem=sems[0].at[slot],
        recv_sem=sems[1].at[slot],
        device_id=partner,
        device_id_type=MESH,
    )
    copy.start()
    return copy


def owner_sums_kernel(count, *refs):
    parts, outs, rest = refs[:count], refs[count : 2 * count], refs[2 * count :]
    per = 7
    scratch = [rest[per * i : per * (i + 1)] for i in range(count)]
    sems = rest[per * count :]
    shard, ctx, tp = lax.axis_index("shard"), lax.axis_index("ctx"), lax.axis_index("tp")
    side, core = ctx // 2, ctx % 2
    by_core = (shard, side * 2 + 1 - core, tp)
    by_shard = (1 - shard, ctx, tp)
    by_side = (shard, (1 - side) * 2 + core, tp)
    greet((by_core, by_shard, by_side))
    first = [
        remote(parts[i].at[1 - core], scratch[i][0], sems, 4 * i, by_core) for i in range(count)
    ]
    second, third, fourth = [], [], []
    for i in range(count):
        in_one, send_two, in_two, send_three, in_three, send_four, in_four = scratch[i]
        first[i].wait()
        send_two[...] = (
            parts[i][core, 1 - shard].astype(jnp.float32)
            + in_one[1 - shard].astype(jnp.float32)
        ).astype(jnp.bfloat16)
        second.append(remote(send_two, in_two, sems, 4 * i + 1, by_shard))
    for i in range(count):
        in_one, send_two, in_two, send_three, in_three, send_four, in_four = scratch[i]
        second[i].wait()
        send_three[...] = (
            parts[i][core, shard].astype(jnp.float32)
            + in_one[shard].astype(jnp.float32)
            + in_two[...].astype(jnp.float32)
        ).astype(jnp.bfloat16)
        third.append(remote(send_three, in_three, sems, 4 * i + 2, by_side))
    for i in range(count):
        in_one, send_two, in_two, send_three, in_three, send_four, in_four = scratch[i]
        third[i].wait()
        send_four[...] = (
            send_three[...].astype(jnp.float32) + in_three[...].astype(jnp.float32)
        ).astype(jnp.bfloat16)
        fourth.append(remote(send_four, in_four, sems, 4 * i + 3, by_core))
        outs[i][core] = send_four[...].astype(jnp.float32)
    for i in range(count):
        fourth[i].wait()
        outs[i][1 - core] = scratch[i][6][...].astype(jnp.float32)


def owner_sums(parts, collective):
    scratch = []
    for part in parts:
        piece = pltpu.VMEM(part.shape[2:], jnp.bfloat16)
        scratch += [pltpu.VMEM(part.shape[1:], jnp.bfloat16)] + [piece] * 6
    count = len(parts)
    size = sum(part.size for part in parts)
    vmem = pl.BlockSpec(memory_space=pltpu.VMEM)
    return pl.pallas_call(
        functools.partial(owner_sums_kernel, count),
        in_specs=[vmem] * count,
        out_specs=[vmem] * count,
        out_shape=[
            jax.ShapeDtypeStruct((part.shape[0],) + part.shape[2:], jnp.float32) for part in parts
        ],
        scratch_shapes=scratch + [pltpu.SemaphoreType.DMA((4 * count,))] * 2,
        compiler_params=pltpu.CompilerParams(
            collective_id=collective, has_side_effects=True, vmem_limit_bytes=VMEM_BYTES
        ),
        cost_estimate=pl.CostEstimate(flops=size, bytes_accessed=size * 30, transcendentals=0),
    )(*parts)


def small_sums_kernel(rows_all, vec_ref, out_ref, plane_in, line_out, line_in, sems_a, sems_b):
    shard, ctx, tp = lax.axis_index("shard"), lax.axis_index("ctx"), lax.axis_index("tp")
    n_shard, n_ctx, n_tp = (lax.axis_size(a) for a in ("shard", "ctx", "tp"))
    plane = n_shard * n_ctx
    me = shard * n_ctx + ctx
    partners = []
    for step in range(1, plane):
        other = lax.rem(me + step, plane)
        partners.append((other // n_ctx, lax.rem(other, n_ctx), tp))
    lines = [(shard, ctx, lax.rem(tp + step, n_tp)) for step in range(1, n_tp)]
    greet(partners + lines)
    copies = [
        remote(vec_ref, plane_in.at[step], (sems_a.at[0], sems_a.at[1]), step, partners[step])
        for step in range(plane - 1)
    ]
    for copy in copies:
        copy.wait()
    total = jnp.zeros_like(vec_ref[...])
    for source in range(plane):
        gap = lax.rem(me - source + plane, plane)
        slot = jnp.maximum(gap - 1, 0)
        total += jnp.where(gap == 0, vec_ref[...], plane_in[slot])
    line_out[...] = total[:rows_all]
    copies = [
        remote(line_out, line_in.at[step], (sems_b.at[0], sems_b.at[1]), step, lines[step])
        for step in range(n_tp - 1)
    ]
    out_ref[rows_all:] = total[rows_all:]
    for copy in copies:
        copy.wait()
    total = jnp.zeros_like(line_out[...])
    for source in range(n_tp):
        gap = lax.rem(tp - source + n_tp, n_tp)
        slot = jnp.maximum(gap - 1, 0)
        total += jnp.where(gap == 0, line_out[...], line_in[slot])
    out_ref[:rows_all] = total


def small_sums(vec, rows_all):
    plane = lax.axis_size("shard") * lax.axis_size("ctx")
    n_tp = lax.axis_size("tp")
    vmem = pl.BlockSpec(memory_space=pltpu.VMEM)
    low = (rows_all, vec.shape[1])
    return pl.pallas_call(
        functools.partial(small_sums_kernel, rows_all),
        in_specs=[vmem],
        out_specs=vmem,
        out_shape=jax.ShapeDtypeStruct(vec.shape, jnp.float32),
        scratch_shapes=[
            pltpu.VMEM((plane - 1,) + vec.shape, jnp.float32),
            pltpu.VMEM(low, jnp.float32),
            pltpu.VMEM((n_tp - 1,) + low, jnp.float32),
            pltpu.SemaphoreType.DMA((2, plane - 1)),
            pltpu.SemaphoreType.DMA((2, n_tp - 1)),
        ],
        compiler_params=pltpu.CompilerParams(
            collective_id=7, has_side_effects=True, vmem_limit_bytes=VMEM_BYTES
        ),
        cost_estimate=pl.CostEstimate(flops=vec.size, bytes_accessed=vec.size * 40, transcendentals=0),
    )(vec)


def tp_total(values):
    return lax.psum(values.astype(jnp.bfloat16), "tp").astype(jnp.float32)


def weight_totals(grad_wqkv, grad_wout, grad_wup, grad_wdown):
    low = [g.astype(jnp.bfloat16) for g in (grad_wqkv, grad_wout, grad_wup, grad_wdown)]
    if lax.axis_size("shard") != 2 or lax.axis_size("ctx") != 4:
        return [
            lax.psum(
                lax.psum_scatter(g, "shard", scatter_dimension=dim, tiled=True), "ctx"
            ).astype(jnp.float32)
            for g, dim in zip(low, (1, 1, 0, 1))
        ]
    three, width, local = grad_wqkv.shape
    hidden = grad_wup.shape[1]
    half, quarter = width // 2, width // 4
    up = low[2].reshape(2, 2, quarter, hidden).transpose(1, 0, 2, 3)
    down = low[3].reshape(2, hidden // 2, 2, half).transpose(0, 2, 1, 3)
    up, down = owner_sums((up, down), 3)
    qkv = low[0].reshape(three, 2, 2, quarter, local).transpose(2, 1, 0, 3, 4)
    out = low[1].reshape(2, local // 2, 2, half).transpose(0, 2, 1, 3)
    qkv, out = owner_sums((qkv.reshape(2, 2, three * quarter, local), out), 4)
    qkv = qkv.reshape(2, three, quarter, local).transpose(1, 0, 2, 3).reshape(three, half, local)
    return [
        qkv,
        out.reshape(local, half),
        up.reshape(half, hidden),
        down.reshape(hidden, half),
    ]


def shards(
    inputs,
    cotangent,
    ln1_gain,
    ln1_bias,
    w_qkv,
    q_bias,
    v_bias,
    w_out,
    out_bias,
    ln2_gain,
    ln2_bias,
    w_up,
    up_bias,
    w_down,
    down_bias,
):
    clip_count, block_len, model_width = inputs.shape
    count_of_rows = clip_count * block_len
    share_rows = count_of_rows // lax.axis_size("tp")
    share_start = lax.axis_index("tp") * share_rows

    def rows_part(values):
        return lax.dynamic_slice_in_dim(values, share_start, share_rows, 0)

    wqkv_full, wout_full, wup_full, wdown_full = (
        lax.all_gather(w_qkv, "shard", axis=1, tiled=True),
        lax.all_gather(w_out, "shard", axis=1, tiled=True),
        lax.all_gather(w_up, "shard", axis=0, tiled=True),
        lax.all_gather(w_down, "shard", axis=1, tiled=True),
    )
    shard_local_width = wqkv_full.shape[2]
    x_rows = inputs.astype(jnp.float32).reshape(count_of_rows, model_width)
    normed_one, unit_one, inv_one = norm_rows(x_rows, ln1_gain, ln1_bias)
    act_one = normed_one.astype(jnp.bfloat16)
    projected = jnp.einsum("rd,kdc->krc", act_one, wqkv_full, preferred_element_type=jnp.float32)
    queries = (projected[0] + q_bias).astype(jnp.bfloat16)
    key_rows = projected[1].astype(jnp.bfloat16)
    value_rows = (projected[2] + v_bias).astype(jnp.bfloat16)
    q_blocks = queries.reshape(clip_count, block_len, shard_local_width)
    key_values = jnp.concatenate([key_rows, value_rows], -1)
    key_values = lax.all_gather(
        key_values.reshape(clip_count, block_len, 2 * shard_local_width), "ctx", axis=0
    )
    attn_blocks, attn_cols, log_norm = attend(q_blocks, key_values)
    attn_low = attn_blocks.reshape(count_of_rows, shard_local_width)
    attn_term = jnp.dot(attn_low, wout_full, preferred_element_type=jnp.float32)
    residual = x_rows + tp_total(attn_term) + out_bias
    normed_two, unit_two, inv_two = norm_rows(residual, ln2_gain, ln2_bias)
    act_two = normed_two.astype(jnp.bfloat16)
    hidden_pre = jnp.dot(act_two, wup_full, preferred_element_type=jnp.float32) + up_bias
    hidden = jax.nn.gelu(hidden_pre, approximate=False).astype(jnp.bfloat16)
    branch_term = jnp.dot(hidden, wdown_full, preferred_element_type=jnp.float32)
    grad_y = cotangent.astype(jnp.float32).reshape(count_of_rows, model_width)
    grad_db = jnp.sum(rows_part(grad_y), 0)
    grad_ylow = grad_y.astype(jnp.bfloat16)
    grad_wdown = jnp.einsum("rf,rd->fd", hidden, grad_ylow, preferred_element_type=jnp.float32)
    grad_hidden = jnp.einsum("rd,fd->rf", grad_ylow, wdown_full, preferred_element_type=jnp.float32)
    grad_pre = (grad_hidden * gelu_slope(hidden_pre)).astype(jnp.bfloat16)
    grad_ub = jnp.sum(grad_pre.astype(jnp.float32), 0)
    grad_wup = jnp.einsum("rd,rf->df", act_two, grad_pre, preferred_element_type=jnp.float32)
    acttwo_term = jnp.einsum("rf,df->rd", grad_pre, wup_full, preferred_element_type=jnp.float32)
    grad_acttwo = tp_total(acttwo_term)
    grad_acttwo, branch_term = lax.optimization_barrier((grad_acttwo, branch_term.astype(jnp.bfloat16)))
    branch_total = lax.psum(branch_term, "tp").astype(jnp.float32)
    output = (
        (residual + branch_total + down_bias)
        .astype(jnp.bfloat16)
        .reshape(clip_count, block_len, model_width)
    )
    grad_resid = grad_y + norm_back(grad_acttwo, unit_two, inv_two, ln2_gain)
    grad_g2 = jnp.sum(rows_part(grad_acttwo) * rows_part(unit_two), 0)
    grad_b2 = jnp.sum(rows_part(grad_acttwo), 0)
    grad_ob = jnp.sum(rows_part(grad_resid), 0)
    grad_mixed = grad_resid.astype(jnp.bfloat16)
    grad_wout = jnp.einsum("rc,rd->cd", attn_low, grad_mixed, preferred_element_type=jnp.float32)
    grad_attn = jnp.einsum(
        "rd,cd->rc", grad_mixed, wout_full, preferred_element_type=jnp.float32
    ).astype(jnp.bfloat16)
    grad_query, grad_kv = attend_back(
        q_blocks,
        key_values,
        grad_attn.reshape(clip_count, block_len, shard_local_width),
        attn_cols,
        log_norm,
    )
    key_value_totals = lax.psum_scatter(grad_kv, "ctx", scatter_dimension=0, tiled=False)
    key_value_totals = key_value_totals.reshape(count_of_rows, 2 * shard_local_width)
    query_gradient_partial = grad_query.reshape(count_of_rows, shard_local_width)
    key_gradient_partial = key_value_totals[:, :shard_local_width]
    value_gradient_partial = key_value_totals[:, shard_local_width:]
    three = (query_gradient_partial, key_gradient_partial, value_gradient_partial)
    grad_qb = jnp.sum(query_gradient_partial.astype(jnp.float32), 0)
    grad_vb = jnp.sum(value_gradient_partial.astype(jnp.float32), 0)
    grad_wqkv = jnp.stack(
        [jnp.einsum("rd,rc->dc", act_one, part, preferred_element_type=jnp.float32) for part in three]
    )
    actone_term = sum(
        jnp.einsum("rc,dc->rd", part, wqkv_full[i], preferred_element_type=jnp.float32)
        for i, part in enumerate(three)
    )
    actone_term, output = lax.optimization_barrier((actone_term, output))
    grad_actone = tp_total(actone_term)
    input_norm = norm_back(grad_actone, unit_one, inv_one, ln1_gain)
    grad_g1 = jnp.sum(rows_part(grad_actone) * rows_part(unit_one), 0)
    grad_b1 = jnp.sum(rows_part(grad_actone), 0)
    grad_inputs = (
        (grad_resid + input_norm).astype(jnp.bfloat16).reshape(clip_count, block_len, model_width)
    )
    owned = weight_totals(grad_wqkv, grad_wout, grad_wup, grad_wdown)
    norm_rows_six = jnp.stack([grad_g1, grad_b1, grad_ob, grad_g2, grad_b2, grad_db])
    hidden_width = grad_ub.shape[0]
    if hidden_width == model_width and 2 * shard_local_width <= model_width:
        pad = jnp.zeros((model_width - 2 * shard_local_width,), jnp.float32)
        packed = jnp.concatenate(
            [
                norm_rows_six,
                jnp.zeros((2, model_width), jnp.float32),
                grad_ub[None],
                jnp.concatenate([grad_qb, grad_vb, pad])[None],
                jnp.zeros((6, model_width), jnp.float32),
            ]
        )
        summed = small_sums(packed, 8)
        norm_sums = summed[:6]
        vectors = (
            summed[9, :shard_local_width],
            summed[9, shard_local_width : 2 * shard_local_width],
            summed[8],
        )
    else:
        vectors = lax.psum((grad_qb, grad_vb, grad_ub), ("shard", "ctx"))
        norm_sums = lax.psum(norm_rows_six, ("shard", "ctx", "tp"))
    return (
        output,
        grad_inputs,
        norm_sums[0],
        norm_sums[1],
        owned[0],
        vectors[0],
        vectors[1],
        owned[1],
        norm_sums[2],
        norm_sums[3],
        norm_sums[4],
        owned[2],
        vectors[2],
        owned[3],
        norm_sums[5],
    )


def solution(mesh):
    placed = (
        P("shard", "ctx", None),
        P("shard", "ctx", None),
        P(),
        P(),
        P(None, "shard", "tp"),
        P("tp"),
        P("tp"),
        P("tp", "shard"),
        P(),
        P(),
        P(),
        P("shard", "tp"),
        P("tp"),
        P("tp", "shard"),
        P(),
    )
    return jax.shard_map(
        shards,
        mesh=mesh,
        in_specs=placed,
        out_specs=(
            P("shard", "ctx", None),
            P("shard", "ctx", None),
            P(),
            P(),
            P(None, "shard", "tp"),
            P("tp"),
            P("tp"),
            P("tp", "shard"),
            P(),
            P(),
            P(),
            P("shard", "tp"),
            P("tp"),
            P("tp", "shard"),
            P(),
        ),
        check_vma=False,
    )
```

time: 546 us -> 420 us (0.77); the launches traced: 536 us -> 419 us
  Pallas kernels: 0 us -> 82.9 us
  waiting for transfers between devices: 251 us -> 195 us
  blocking collectives: 74.8 us -> 19.7 us
  local copies, waits for them, and re-layouts: 67.2 us -> 26.5 us
  matrix products: 76.7 us -> 45 us
  other arithmetic: 48.6 us -> 32.1 us
    psum x3, waiting for transfers between devices: 208 us -> 116 us  [tp_total(): return lax.psum(values.astype(jnp.bfloat16), 'tp').astype(jnp.float32)]
    pallas_call x0 -> x5, Pallas kernels: none -> 82.9 us  [the longest x2 51.8 us: owner_sums(): pl.pallas_call(functools.partial(owner_sums_kernel, count), in_specs=[vme...]
    psum x2 -> x0, blocking collectives: 55.2 us -> none  [the longest x1 41 us: shards(): lax.psum((grad_g1, grad_b1, grad_ob, grad_g2, grad_b2, grad_db), ('shard'...]
    unnamed x109 -> x89, local copies, waits for them, and re-layouts: 43.8 us -> 9.3 us
    dot_general x7 -> x6, matrix products: 40.2 us -> 12.3 us  [the longest x3 7.25 us: shards(): jnp.einsum('rc,dc->rd', part, wqkv_full[i], preferred_element_type=jnp.fl...]
    psum x1, waiting for transfers between devices: 0.01 us -> 26.8 us  [shards(): branch_total = lax.psum(branch_term, 'tp').astype(jnp.float32)]
    reduce_scatter x1, waiting for transfers between devices: 16.1 us -> 31.8 us  [shards(): lax.psum_scatter(grad_kv, 'ctx', scatter_dimension=0, tiled=False)]
    unnamed x17 -> x8, waiting for transfers between devices: 12.9 us -> 1.15 us
  transfers between devices with their start and end apart: 13 -> 8, of which waited for: 7 -> 6; matrix products, arithmetic and copies ran while one was open for 22% -> 12% of each run, Pallas kernels for 0% -> 10%
where the time goes in v1:
time: 420 us; the launch traced here: 419 us
  waiting for transfers between devices  195 us (46%)
  Pallas kernels  82.9 us (20%)
  matrix products  45 us (11%)
  other arithmetic  32.1 us (8%)
  local copies, waits for them, and re-layouts  26.5 us (6%)
  blocking collectives  19.7 us (5%)
  between operations  16.3 us (4%)
    psum x3, waiting for transfers between devices, tp_total(): return lax.psum(values.astype(jnp.bfloat16), 'tp').astype(jnp.float32)  116 us
    pallas_call x2, Pallas kernels, owner_sums(): pl.pallas_call(functools.partial(owner_sums_kernel, count), in_specs=[vme...  51.8 us
    reduce_scatter x1, waiting for transfers between devices, shards(): lax.psum_scatter(grad_kv, 'ctx', scatter_dimension=0, tiled=False)  31.8 us
    psum x1, waiting for transfers between devices, shards(): branch_total = lax.psum(branch_term, 'tp').astype(jnp.float32)  26.8 us
    all_gather x1, waiting for transfers between devices, shards(): lax.all_gather(key_values.reshape(clip_count, block_len, 2 * shard_local_...  19.4 us
    all_gather x1, blocking collectives, shards(): lax.all_gather(w_qkv, 'shard', axis=1, tiled=True)  13.8 us
    pallas_call x1, Pallas kernels, small_sums(): pl.pallas_call(functools.partial(small_sums_kernel, rows_all), in_specs=[...  12.6 us
    pallas_call x1, Pallas kernels, attend_back(): pl.pallas_call(attend_back_kernel, grid=(clips,), in_specs=[row, wide, ro...  11.7 us
  transfers between devices with their start and end apart: 8, of which 6 were waited for; matrix products, arithmetic and copies ran while one was open for 12% of the time, Pallas kernels for 10%

profile of v1, /device:TPU:0, one launch (start us, length us, event | category | flops | bytes accessed | tf_op | source)
XLA Modules:
  0.0 418.7 jit_solution(430909640761255617)
XLA Ops:
  11.5 13.8 %all_gather.15 = bf16[3,768,192]{1,2,0:T(8,128)(2,1)S(1)} all-gather(bf16[3,384,192]{1,2,0:T(8,128)(2,1)S(1)} %copy-done.20), channel_id=1, replica_groups=mesh['shard'=2,'ctx'=4,'tp'=4] {'shard'}, dimensions={1}, use_global_device_ids=true | all-gather | bytes 1327104 | tf_op jit(solution)/shard_map/all_gather | solution.py:363
  29.5 5.9 %all_gather.17 = bf16[192,768]{1,0:T(8,128)(2,1)} all-gather(bf16[192,384]{1,0:T(8,128)(2,1)S(1)} %copy-done.22), channel_id=1, replica_groups=mesh['shard'=2,'ctx'=4,'tp'=4] {'shard'}, dimensions={1}, use_global_device_ids=true | all-gather | bytes 442368 | tf_op jit(solution)/shard_map/all_gather | solution.py:364
  35.5 19.4 %all-gather.4.cloned.1.call-done.kv_ref = bf16[4,2,384,384]{3,2,1,0:T(8,128)(2,1)} async-done(((bf16[1,2,384,384]{3,2,1,0:T(8,128)(2,1)}), bf16[4,2,384,384]{3,2,1,0:T(8,128)(2,1)}) %all-gather.4.cloned.1.call-update) | async-done | bytes 2359312 | tf_op jit(solution)/shard_map/all_gather | solution.py:378
  56.5 6.8 %shard_map.262 = (bf16[2,384,192]{2,1,0:T(8,128)(2,1)S(1)}, f32[2,192,384]{2,1,0:T(8,128)S(1)}, f32[2,8,384]{2,1,0:T(8,128)S(1)}) custom-call(bf16[2,384,192]{2,1,0:T(8,128)(2,1)S(1)} %add_convert_fusion.4.q_ref, bf16[4,2,384,384]{3,2,1,0:T(8,128)(2,1)S(1)} %copy-done.2), custom_call_target="tpu_custom_call" | custom-call | flops 905969664 | bytes 2949120 | tf_op jit(solution)/shard_map/pallas_call | solution.py:81
  66.2 54.7 %all-reduce.5.cloned.1.call-done = bf16[768,768]{1,0:T(8,128)(2,1)} async-done(((bf16[768,768]{1,0:T(8,128)(2,1)}), bf16[768,768]{1,0:T(8,128)(2,1)}) %all-reduce.5.cloned.1.call-update) | async-done | bytes 1179664 | tf_op jit(solution)/shard_map/psum | solution.py:307
  125.3 8.7 %fusion.8 = (bf16[768,768]{1,0:T(8,128)(2,1)}, f32[768,768]{1,0:T(8,128)}) fusion(f32[768]{0:T(1024)} %param.27, bf16[768,768]{1,0:T(8,128)(2,1)} %all-gather.8.cloned.1.call-done, f32[768,768]{1,0:T(8,128)} %subtract_multiply_fusion, f32[768]{0:T(1024)} %param.25, f32[768]{0:T(1024)} %param.24), kind=kOutput, calls=%fused_computation.10 | convolution fusion | flops 946667520 | bytes 7087104 | tf_op jit(solution)/shard_map/dot_general | solution.py:387
  134.1 4.0 convert_reduce_fusion.1
  141.3 3.7 convolution_convert_fusion.2
  145.0 51.8 %all-reduce.7.cloned.1.call-done = bf16[768,768]{1,0:T(8,128)(2,1)} async-done(((bf16[768,768]{1,0:T(8,128)(2,1)}), bf16[768,768]{1,0:T(8,128)(2,1)}) %all-reduce.7.cloned.1.call-update) | async-done | bytes 1179664 | tf_op jit(solution)/shard_map/psum | solution.py:307
  200.1 3.0 multiply_reduce_fusion.4
  205.9 2.9 convolution_convert_fusion.8
  210.0 11.7 %shard_map.263 = (bf16[2,384,192]{2,1,0:T(8,128)(2,1)S(1)}, bf16[4,2,384,384]{3,2,1,0:T(8,128)(2,1)}) custom-call(bf16[2,384,192]{2,1,0:T(8,128)(2,1)S(1)} %add_convert_fusion.4.q_ref, bf16[4,2,384,384]{3,2,1,0:T(8,128)(2,1)} %all-gather.4.cloned.1.call-done.kv_ref, bf16[2,384,192]{2,1,0:T(8,128)(2,1)S(1)} %bitcast.130, ...), custom_call_target="tpu_custom_call" | custom-call | flops 2264924160 | bytes 5898240 | tf_op jit(solution)/shard_map/pallas_call | solution.py:133
  222.5 3.1 convolution_convert_fusion.1
  228.6 26.8 %all-reduce.9.cloned.1.call-done = bf16[768,768]{1,0:T(8,128)(2,1)} async-done(((bf16[768,768]{1,0:T(8,128)(2,1)}), bf16[768,768]{1,0:T(8,128)(2,1)}) %all-reduce.9.cloned.1.call-update) | async-done | bytes 1179664 | tf_op jit(solution)/shard_map/psum | solution.py:401
  255.4 3.2 add_convert_fusion.1
  258.6 31.8 %reduce-scatter.2.cloned.1.call-done = bf16[1,2,384,384]{3,2,1,0:T(8,128)(2,1)} async-done(((bf16[4,2,384,384]{3,2,1,0:T(8,128)(2,1)}), bf16[1,2,384,384]{3,2,1,0:T(8,128)(2,1)}) %reduce-scatter.2.cloned.1.call-update) | async-done | bytes 589840 | tf_op jit(solution)/shard_map/reduce_scatter | solution.py:423
  295.1 3.4 convolution_convert_fusion
  302.4 29.0 %shard_map.266 = (f32[2,192,768]{2,1,0:T(8,128)S(1)}, f32[2,384,384]{2,1,0:T(8,128)S(1)}) custom-call(bf16[2,2,192,768]{3,2,1,0:T(8,128)(2,1)S(1)} %bitcast.121, bf16[2,2,384,384]{3,2,1,0:T(8,128)(2,1)} %bitcast.134), custom_call_target="tpu_custom_call" | custom-call | flops 1179648 | bytes 35389440 | tf_op jit(solution)/shard_map/pallas_call | solution.py:229
  341.2 9.9 %all-reduce.11.cloned.1.call-done = bf16[768,768]{1,0:T(8,128)(2,1)} async-done(((bf16[768,768]{1,0:T(8,128)(2,1)}), bf16[768,768]{1,0:T(8,128)(2,1)}) %all-reduce.11.cloned.1.call-update) | async-done | bytes 1179664 | tf_op jit(solution)/shard_map/psum | solution.py:307
  354.1 12.6 %shard_map.264 = f32[16,768]{1,0:T(8,128)S(1)} custom-call(f32[16,768]{1,0:T(8,128)S(1)} %concatenate.14.vec_ref), custom_call_target="tpu_custom_call" | custom-call | flops 12288 | bytes 491520 | tf_op jit(solution)/shard_map/pallas_call | solution.py:287
  368.0 3.2 multiply_reduce_fusion.3
  377.7 22.8 %shard_map.265 = (f32[2,576,192]{2,1,0:T(8,128)S(1)}, f32[2,96,384]{2,1,0:T(8,128)S(1)}) custom-call(bf16[2,2,576,192]{3,2,1,0:T(8,128)(2,1)S(1)} %bitcast.122, bf16[2,2,96,384]{3,2,1,0:T(8,128)(2,1)S(1)} %bitcast.129), custom_call_target="tpu_custom_call" | custom-call | flops 589824 | bytes 17694720 | tf_op jit(solution)/shard_map/pallas_call | solution.py:229
  402.0 3.2 reshape.239
  405.2 3.3 add_convert_fusion
  (176 shorter events, 63.5 us)
Async XLA Ops:
  8.0 17.3 %copy-start.3 = (bf16[2,384,768]{2,1,0:T(8,128)(2,1)S(1)}, bf16[2,384,768]{2,1,0:T(8,128)(2,1)}, u32[]{:S(2)}) copy-start(bf16[2,384,768]{2,1,0:T(8,128)(2,1)} %param.15) | copy-start | bytes 3538948
  8.0 46.8 %all-gather.4.cloned.1.call-start = ((), (), s32[]{:S(2)}) async-start(), calls=%async_computation.1 | async-start | bytes 2949120 | tf_op jit(solution)/shard_map/all_gather | solution.py:378
  9.7 16.0 %copy-start.24 = (f32[2,384]{1,0:T(2,128)}, f32[2,384]{1,0:T(2,128)S(1)}, u32[]{:S(2)}) copy-start(f32[2,384]{1,0:T(2,128)S(1)} %broadcast_multiply_fusion.5) | copy-start | bytes 9220
  11.5 14.3 %copy-start.30 = (f32[2,384]{1,0:T(2,128)}, f32[2,384]{1,0:T(2,128)S(1)}, u32[]{:S(2)}) copy-start(f32[2,384]{1,0:T(2,128)S(1)} %add_rsqrt_fusion.1) | copy-start | bytes 9220
  11.5 14.3 %copy-start.26 = (f32[768]{0:T(1024)S(1)}, f32[768]{0:T(1024)}, u32[]{:S(2)}) copy-start(f32[768]{0:T(1024)} %param.17) | copy-start | bytes 9220
  11.5 14.2 %copy-start.33 = (f32[768]{0:T(1024)S(1)}, f32[768]{0:T(1024)}, u32[]{:S(2)}) copy-start(f32[768]{0:T(1024)} %param.18) | copy-start | bytes 9220
  28.0 7.4 %copy-start.37 = (f32[192]{0:T(256)S(1)}, f32[192]{0:T(256)}, u32[]{:S(2)}) copy-start(f32[192]{0:T(256)} %param.20) | copy-start | bytes 2308
  29.2 91.7 %all-reduce.5.cloned.1.call-start = ((), (), s32[]{:S(2)}) async-start(), calls=%async_computation.2 | async-start | bytes 2359296 | tf_op jit(solution)/shard_map/psum | solution.py:307
  56.5 6.8 %copy-start.15 = (bf16[192,768]{1,0:T(8,128)(2,1)S(1)}, bf16[192,768]{1,0:T(8,128)(2,1)}, u32[]{:S(2)}) copy-start(bf16[192,768]{1,0:T(8,128)(2,1)} %all_gather.17) | copy-start | bytes 884740
  63.3 57.6 %copy-start.23 = (f32[768]{0:T(1024)S(1)}, f32[768]{0:T(1024)}, u32[]{:S(2)}) copy-start(f32[768]{0:T(1024)} %param.23) | copy-start | bytes 9220
  64.8 60.5 %all-gather.8.cloned.1.call-start = ((), (), s32[]{:S(2)}) async-start(), calls=%async_computation.4 | async-start | bytes 1769472 | tf_op jit(solution)/shard_map/all_gather | solution.py:365
  65.4 68.6 %all-gather.6.cloned.1.call-start = ((), (), s32[]{:S(2)}) async-start(), calls=%async_computation.3 | async-start | bytes 1769472 | tf_op jit(solution)/shard_map/all_gather | solution.py:366
  66.0 130.9 %all-reduce.7.cloned.1.call-start = ((), (), s32[]{:S(2)}) async-start(), calls=%async_computation.5 | async-start | bytes 2359296 | tf_op jit(solution)/shard_map/psum | solution.py:307
  125.3 8.7 %copy-start.11 = (bf16[2,384,768]{2,1,0:T(8,128)(2,1)S(1)}, bf16[2,384,768]{2,1,0:T(8,128)(2,1)}, u32[]{:S(2)}) copy-start(bf16[2,384,768]{2,1,0:T(8,128)(2,1)} %param.16) | copy-start | bytes 3538948
  125.3 8.7 %copy-start.39 = (f32[768]{0:T(1024)S(1)}, f32[768]{0:T(1024)}, u32[]{:S(2)}) copy-start(f32[768]{0:T(1024)} %param.27) | copy-start | bytes 9220
  141.3 114.1 %all-reduce.9.cloned.1.call-start = ((), (), s32[]{:S(2)}) async-start(), calls=%async_computation.7 | async-start | bytes 2359296 | tf_op jit(solution)/shard_map/psum | solution.py:401
  145.0 55.0 %copy-start.28 = (f32[768]{0:T(1024)S(1)}, f32[768]{0:T(1024)}, u32[]{:S(2)}) copy-start(f32[768]{0:T(1024)} %param.24) | copy-start | bytes 9220
  199.8 90.6 %reduce-scatter.2.cloned.1.call-start = ((), (), s32[]{:S(2)}) async-start(), calls=%async_computation.6 | async-start | bytes 2949120 | tf_op jit(solution)/shard_map/reduce_scatter | solution.py:423
  221.8 129.4 %all-reduce.11.cloned.1.call-start = ((), (), s32[]{:S(2)}) async-start(), calls=%async_computation.8 | async-start | bytes 2359296 | tf_op jit(solution)/shard_map/psum | solution.py:307
  225.6 29.8 %copy-start.4 = (bf16[2,384,768]{2,1,0:T(8,128)(2,1)S(1)}, bf16[2,384,768]{2,1,0:T(8,128)(2,1)}, u32[]{:S(2)}) copy-start(bf16[2,384,768]{2,1,0:T(8,128)(2,1)} %param.15) | copy-start | bytes 3538948
  225.6 29.8 %copy-start.32 = (f32[768]{0:T(1024)S(1)}, f32[768]{0:T(1024)}, u32[]{:S(2)}) copy-start(f32[768]{0:T(1024)} %param.29) | copy-start | bytes 9220
  333.8 5.3 %copy-start.5 = (bf16[2,384,768]{2,1,0:T(8,128)(2,1)S(1)}, bf16[2,384,768]{2,1,0:T(8,128)(2,1)}, u32[]{:S(2)}) copy-start(bf16[2,384,768]{2,1,0:T(8,128)(2,1)} %param.15) | copy-start | bytes 3538948
  333.8 5.3 %copy-start.25 = (f32[2,384]{1,0:T(2,128)S(1)}, f32[2,384]{1,0:T(2,128)}, u32[]{:S(2)}) copy-start(f32[2,384]{1,0:T(2,128)} %copy-done.24) | copy-start | bytes 9220
  341.2 12.6 %copy-start.21 = (bf16[768,192]{0,1:T(8,128)(2,1)S(1)}, bf16[768,192]{0,1:T(8,128)(2,1)}, u32[]{:S(2)}) copy-start(bf16[768,192]{0,1:T(8,128)(2,1)} %fusion.25) | copy-start | bytes 884740
  (26 other events, 63.8 us)
Sparse Core Ops, SparseCore 0:
  29.3 25.5 all-gather.3
  65.0 55.8 all-reduce.4
  141.4 55.4 all-reduce.6
  199.9 55.4 all-reduce.8
  257.8 32.5 reduce-scatter.1
  295.2 55.9 all-reduce.10
Sparse Core Ops, SparseCore 1:
  66.8 22.6 all-gather.7
  90.9 22.7 all-gather.5

commit v2 on v1

--- a/solution.py
+++ b/solution.py
@@ -173,56 +173,88 @@
     return copy
 
 
+def places():
+    shard, ctx, tp = lax.axis_index("shard"), lax.axis_index("ctx"), lax.axis_index("tp")
+    side, core = ctx // 2, ctx % 2
+    by_core = (shard, side * 2 + 1 - core, tp)
+    by_shard = (1 - shard, ctx, tp)
+    by_side = (shard, (1 - side) * 2 + core, tp)
+    return shard, side, core, by_core, by_shard, by_side
+
+
+def in_pairs():
+    return lax.axis_size("shard") == 2 and lax.axis_size("ctx") == 4
+
+
+def piece_of(ref, shard, core):
+    if len(ref.shape) == 4:
+        return ref.at[shard, core]
+    half = ref.shape[2] // 2
+    return ref.at[core, :, pl.ds(pl.multiple_of(shard * half, half), half)]
+
+
+def piece_shape(part):
+    if part.ndim == 4:
+        return part.shape[2:]
+    return (part.shape[1], part.shape[2] // 2)
+
+
+def wide_f32(ref):
+    return ref[...].astype(jnp.float32)
+
+
 def owner_sums_kernel(count, *refs):
     parts, outs, rest = refs[:count], refs[count : 2 * count], refs[2 * count :]
     per = 7
     scratch = [rest[per * i : per * (i + 1)] for i in range(count)]
     sems = rest[per * count :]
-    shard, ctx, tp = lax.axis_index("shard"), lax.axis_index("ctx"), lax.axis_index("tp")
-    side, core = ctx // 2, ctx % 2
-    by_core = (shard, side * 2 + 1 - core, tp)
-    by_shard = (1 - shard, ctx, tp)
-    by_side = (shard, (1 - side) * 2 + core, tp)
+    shard, side, core, by_core, by_shard, by_side = places()
     greet((by_core, by_shard, by_side))
-    first = [
-        remote(parts[i].at[1 - core], scratch[i][0], sems, 4 * i, by_core) for i in range(count)
-    ]
+    first = []
+    for i in range(count):
+        for slot, owner in enumerate((1 - shard, shard)):
+            first.append(
+                remote(
+                    piece_of(parts[i], owner, 1 - core),
+                    scratch[i][0].at[slot],
+                    sems,
+                    5 * i + slot,
+                    by_core,
+                )
+            )
     second, third, fourth = [], [], []
     for i in range(count):
         in_one, send_two, in_two, send_three, in_three, send_four, in_four = scratch[i]
-        first[i].wait()
+        first[2 * i].wait()
         send_two[...] = (
-            parts[i][core, 1 - shard].astype(jnp.float32)
-            + in_one[1 - shard].astype(jnp.float32)
+            wide_f32(piece_of(parts[i], 1 - shard, core)) + wide_f32(in_one.at[0])
         ).astype(jnp.bfloat16)
-        second.append(remote(send_two, in_two, sems, 4 * i + 1, by_shard))
+        second.append(remote(send_two, in_two, sems, 5 * i + 2, by_shard))
     for i in range(count):
         in_one, send_two, in_two, send_three, in_three, send_four, in_four = scratch[i]
+        first[2 * i + 1].wait()
         second[i].wait()
         send_three[...] = (
-            parts[i][core, shard].astype(jnp.float32)
-            + in_one[shard].astype(jnp.float32)
-            + in_two[...].astype(jnp.float32)
+            wide_f32(piece_of(parts[i], shard, core)) + wide_f32(in_one.at[1]) + wide_f32(in_two)
         ).astype(jnp.bfloat16)
-        third.append(remote(send_three, in_three, sems, 4 * i + 2, by_side))
+        third.append(remote(send_three, in_three, sems, 5 * i + 3, by_side))
     for i in range(count):
         in_one, send_two, in_two, send_three, in_three, send_four, in_four = scratch[i]
         third[i].wait()
-        send_four[...] = (
-            send_three[...].astype(jnp.float32) + in_three[...].astype(jnp.float32)
-        ).astype(jnp.bfloat16)
-        fourth.append(remote(send_four, in_four, sems, 4 * i + 3, by_core))
-        outs[i][core] = send_four[...].astype(jnp.float32)
+        send_four[...] = (wide_f32(send_three) + wide_f32(in_three)).astype(jnp.bfloat16)
+        fourth.append(remote(send_four, in_four, sems, 5 * i + 4, by_core))
+        outs[i][core] = wide_f32(send_four)
     for i in range(count):
         fourth[i].wait()
-        outs[i][1 - core] = scratch[i][6][...].astype(jnp.float32)
+        outs[i][1 - core] = wide_f32(scratch[i][6])
 
 
 def owner_sums(parts, collective):
     scratch = []
     for part in parts:
-        piece = pltpu.VMEM(part.shape[2:], jnp.bfloat16)
-        scratch += [pltpu.VMEM(part.shape[1:], jnp.bfloat16)] + [piece] * 6
+        shape = piece_shape(part)
+        scratch += [pltpu.VMEM((2,) + shape, jnp.bfloat16)]
+        scratch += [pltpu.VMEM(shape, jnp.bfloat16)] * 6
     count = len(parts)
     size = sum(part.size for part in parts)
     vmem = pl.BlockSpec(memory_space=pltpu.VMEM)
@@ -230,15 +262,171 @@
         functools.partial(owner_sums_kernel, count),
         in_specs=[vmem] * count,
         out_specs=[vmem] * count,
-        out_shape=[
-            jax.ShapeDtypeStruct((part.shape[0],) + part.shape[2:], jnp.float32) for part in parts
-        ],
-        scratch_shapes=scratch + [pltpu.SemaphoreType.DMA((4 * count,))] * 2,
+        out_shape=[jax.ShapeDtypeStruct((2,) + piece_shape(part), jnp.float32) for part in parts],
+        scratch_shapes=scratch + [pltpu.SemaphoreType.DMA((5 * count,))] * 2,
         compiler_params=pltpu.CompilerParams(
             collective_id=collective, has_side_effects=True, vmem_limit_bytes=VMEM_BYTES
         ),
         cost_estimate=pl.CostEstimate(flops=size, bytes_accessed=size * 30, transcendentals=0),
     )(*parts)
+
+
+def kv_gather_kernel(own_ref, all_ref, send_sem, recv_sem):
+    shard, side, core, by_core, by_shard, by_side = places()
+    clips = own_ref.shape[0]
+    sems = (send_sem, recv_sem)
+    mine, across = side * 2 + core, (1 - side) * 2 + core
+    greet((by_core, by_side))
+    sent = [
+        remote(own_ref.at[c], all_ref.at[mine, c], sems, c, by_side) for c in range(clips)
+    ]
+    near = remote(own_ref, all_ref.at[mine], sems, 2 * clips, by_core)
+    all_ref[mine] = own_ref[...]
+    passed = []
+    for c in range(clips):
+        sent[c].wait()
+        passed.append(
+            remote(all_ref.at[across, c], all_ref.at[across, c], sems, clips + c, by_core)
+        )
+    near.wait()
+    for copy in passed:
+        copy.wait()
+
+
+def kv_gather(own):
+    if not in_pairs():
+        return lax.all_gather(own, "ctx", axis=0)
+    vmem = pl.BlockSpec(memory_space=pltpu.VMEM)
+    return pl.pallas_call(
+        kv_gather_kernel,
+        in_specs=[vmem],
+        out_specs=vmem,
+        out_shape=jax.ShapeDtypeStruct((4,) + own.shape, own.dtype),
+        scratch_shapes=[pltpu.SemaphoreType.DMA((2 * own.shape[0] + 1,))] * 2,
+        compiler_params=pltpu.CompilerParams(
+            collective_id=8, has_side_effects=True, vmem_limit_bytes=VMEM_BYTES
+        ),
+        cost_estimate=pl.CostEstimate(flops=0, bytes_accessed=own.size * 80, transcendentals=0),
+    )(own)
+
+
+def kv_scatter_kernel(all_ref, own_ref, in_core, send_side, in_side, send_sem, recv_sem):
+    shard, side, core, by_core, by_shard, by_side = places()
+    clips = own_ref.shape[0]
+    sems = (send_sem, recv_sem)
+    greet((by_core, by_side))
+    near = [
+        remote(
+            all_ref.at[owner * 2 + 1 - core, c], in_core.at[slot, c], sems, slot * clips + c, by_core
+        )
+        for slot, owner in enumerate((1 - side, side))
+        for c in range(clips)
+    ]
+    far = []
+    for c in range(clips):
+        near[c].wait()
+        send_side[c] = (
+            wide_f32(all_ref.at[(1 - side) * 2 + core, c]) + wide_f32(in_core.at[0, c])
+        ).astype(jnp.bfloat16)
+        far.append(remote(send_side.at[c], in_side.at[c], sems, 2 * clips + c, by_side))
+    for c in range(clips):
+        near[clips + c].wait()
+        far[c].wait()
+        own_ref[c] = (
+            wide_f32(all_ref.at[side * 2 + core, c])
+            + wide_f32(in_core.at[1, c])
+            + wide_f32(in_side.at[c])
+        ).astype(jnp.bfloat16)
+
+
+def kv_scatter(parts):
+    if not in_pairs():
+        return lax.psum_scatter(parts, "ctx", scatter_dimension=0, tiled=False)
+    vmem = pl.BlockSpec(memory_space=pltpu.VMEM)
+    own = parts.shape[1:]
+    return pl.pallas_call(
+        kv_scatter_kernel,
+        in_specs=[vmem],
+        out_specs=vmem,
+        out_shape=jax.ShapeDtypeStruct(own, parts.dtype),
+        scratch_shapes=[
+            pltpu.VMEM((2,) + own, jnp.bfloat16),
+            pltpu.VMEM(own, jnp.bfloat16),
+            pltpu.VMEM(own, jnp.bfloat16),
+        ]
+        + [pltpu.SemaphoreType.DMA((3 * own[0],))] * 2,
+        compiler_params=pltpu.CompilerParams(
+            collective_id=9, has_side_effects=True, vmem_limit_bytes=VMEM_BYTES
+        ),
+        cost_estimate=pl.CostEstimate(flops=0, bytes_accessed=parts.size * 25, transcendentals=0),
+    )(parts)
+
+
+def weight_gather_kernel(qkv_ref, out_ref, qkv_all, out_all, send_sem, recv_sem):
+    shard, side, core, by_core, by_shard, by_side = places()
+    sems = (send_sem, recv_sem)
+    half, part = qkv_ref.shape[1] // 2, out_ref.shape[0] // 2
+    cols = out_ref.shape[1]
+
+    def qkv_slot(owner):
+        return qkv_all.at[:, owner, pl.ds(pl.multiple_of(core * half, half), half), :]
+
+    def out_slot(owner):
+        return out_all.at[
+            pl.ds(pl.multiple_of(core * part, part), part),
+            pl.ds(pl.multiple_of(owner * cols, cols), cols),
+        ]
+
+    greet((by_core, by_shard))
+    sent = [
+        remote(
+            qkv_ref.at[:, pl.ds(pl.multiple_of(core * half, half), half), :],
+            qkv_slot(shard),
+            sems,
+            0,
+            by_shard,
+        ),
+        remote(
+            out_ref.at[pl.ds(pl.multiple_of(core * part, part), part), :],
+            out_slot(shard),
+            sems,
+            1,
+            by_shard,
+        ),
+    ]
+    qkv_all[:, shard] = qkv_ref[...]
+    out_all[:, pl.ds(pl.multiple_of(shard * cols, cols), cols)] = out_ref[...]
+    sent[0].wait()
+    passed = [remote(qkv_slot(1 - shard), qkv_slot(1 - shard), sems, 2, by_core)]
+    sent[1].wait()
+    passed.append(remote(out_slot(1 - shard), out_slot(1 - shard), sems, 3, by_core))
+    for copy in passed:
+        copy.wait()
+
+
+def weight_gather(w_qkv, w_out):
+    if not in_pairs():
+        return (
+            lax.all_gather(w_qkv, "shard", axis=1, tiled=True),
+            lax.all_gather(w_out, "shard", axis=1, tiled=True),
+        )
+    three, rows, local = w_qkv.shape
+    vmem = pl.BlockSpec(memory_space=pltpu.VMEM)
+    qkv, out = pl.pallas_call(
+        weight_gather_kernel,
+        in_specs=[vmem, vmem],
+        out_specs=[vmem, vmem],
+        out_shape=[
+            jax.ShapeDtypeStruct((three, 2, rows, local), w_qkv.dtype),
+            jax.ShapeDtypeStruct((local, 2 * rows), w_out.dtype),
+        ],
+        scratch_shapes=[pltpu.SemaphoreType.DMA((4,))] * 2,
+        compiler_params=pltpu.CompilerParams(
+            collective_id=10, has_side_effects=True, vmem_limit_bytes=VMEM_BYTES
+        ),
+        cost_estimate=pl.CostEstimate(flops=0, bytes_accessed=w_qkv.size * 60, transcendentals=0),
+    )(w_qkv, w_out)
+    return qkv.reshape(three, 2 * rows, local), out
 
 
 def small_sums_kernel(rows_all, vec_ref, out_ref, plane_in, line_out, line_in, sems_a, sems_b):
@@ -307,31 +495,35 @@
     return lax.psum(values.astype(jnp.bfloat16), "tp").astype(jnp.float32)
 
 
-def weight_totals(grad_wqkv, grad_wout, grad_wup, grad_wdown):
-    low = [g.astype(jnp.bfloat16) for g in (grad_wqkv, grad_wout, grad_wup, grad_wdown)]
-    if lax.axis_size("shard") != 2 or lax.axis_size("ctx") != 4:
-        return [
-            lax.psum(
-                lax.psum_scatter(g, "shard", scatter_dimension=dim, tiled=True), "ctx"
-            ).astype(jnp.float32)
-            for g, dim in zip(low, (1, 1, 0, 1))
-        ]
-    three, width, local = grad_wqkv.shape
-    hidden = grad_wup.shape[1]
-    half, quarter = width // 2, width // 4
-    up = low[2].reshape(2, 2, quarter, hidden).transpose(1, 0, 2, 3)
-    down = low[3].reshape(2, hidden // 2, 2, half).transpose(0, 2, 1, 3)
-    up, down = owner_sums((up, down), 3)
-    qkv = low[0].reshape(three, 2, 2, quarter, local).transpose(2, 1, 0, 3, 4)
-    out = low[1].reshape(2, local // 2, 2, half).transpose(0, 2, 1, 3)
-    qkv, out = owner_sums((qkv.reshape(2, 2, three * quarter, local), out), 4)
-    qkv = qkv.reshape(2, three, quarter, local).transpose(1, 0, 2, 3).reshape(three, half, local)
-    return [
-        qkv,
-        out.reshape(local, half),
-        up.reshape(half, hidden),
-        down.reshape(hidden, half),
-    ]
+def plain_totals(grad, dim):
+    part = lax.psum_scatter(grad, "shard", scatter_dimension=dim, tiled=True)
+    return lax.psum(part, "ctx").astype(jnp.float32)
+
+
+def hidden_totals(grad_wup, grad_wdown):
+    up, down = grad_wup.astype(jnp.bfloat16), grad_wdown.astype(jnp.bfloat16)
+    if not in_pairs():
+        return plain_totals(up, 0), plain_totals(down, 1)
+    width, hidden = up.shape
+    up, down = owner_sums(
+        (up.reshape(2, 2, width // 4, hidden), down.reshape(2, hidden // 2, width)), 3
+    )
+    return up.reshape(width // 2, hidden), down.reshape(hidden, width // 2)
+
+
+def mixer_totals(grad_three, grad_wout):
+    three = [g.astype(jnp.bfloat16) for g in grad_three]
+    out = grad_wout.astype(jnp.bfloat16)
+    if not in_pairs():
+        return plain_totals(jnp.stack(three), 1), plain_totals(out, 1)
+    local, width = out.shape
+    sums = owner_sums(
+        tuple(g.reshape(2, 2, width // 4, local) for g in three)
+        + (out.reshape(2, local // 2, width),),
+        4,
+    )
+    qkv = jnp.stack([g.reshape(width // 2, local) for g in sums[:3]])
+    return qkv, sums[3].reshape(local, width // 2)
 
 
 def shards(
@@ -359,9 +551,8 @@
     def rows_part(values):
         return lax.dynamic_slice_in_dim(values, share_start, share_rows, 0)
 
-    wqkv_full, wout_full, wup_full, wdown_full = (
-        lax.all_gather(w_qkv, "shard", axis=1, tiled=True),
-        lax.all_gather(w_out, "shard", axis=1, tiled=True),
+    wqkv_full, wout_full = weight_gather(w_qkv, w_out)
+    wup_full, wdown_full = (
         lax.all_gather(w_up, "shard", axis=0, tiled=True),
         lax.all_gather(w_down, "shard", axis=1, tiled=True),
     )
@@ -375,8 +566,8 @@
     value_rows = (projected[2] + v_bias).astype(jnp.bfloat16)
     q_blocks = queries.reshape(clip_count, block_len, shard_local_width)
     key_values = jnp.concatenate([key_rows, value_rows], -1)
-    key_values = lax.all_gather(
-        key_values.reshape(clip_count, block_len, 2 * shard_local_width), "ctx", axis=0
+    key_values = kv_gather(
+        key_values.reshape(clip_count, block_len, 2 * shard_local_width)
     )
     attn_blocks, attn_cols, log_norm = attend(q_blocks, key_values)
     attn_low = attn_blocks.reshape(count_of_rows, shard_local_width)
@@ -396,8 +587,12 @@
     grad_ub = jnp.sum(grad_pre.astype(jnp.float32), 0)
     grad_wup = jnp.einsum("rd,rf->df", act_two, grad_pre, preferred_element_type=jnp.float32)
     acttwo_term = jnp.einsum("rf,df->rd", grad_pre, wup_full, preferred_element_type=jnp.float32)
-    grad_acttwo = tp_total(acttwo_term)
-    grad_acttwo, branch_term = lax.optimization_barrier((grad_acttwo, branch_term.astype(jnp.bfloat16)))
+    grad_acttwo = lax.psum(acttwo_term.astype(jnp.bfloat16), "tp")
+    owned_up, owned_down = hidden_totals(grad_wup, grad_wdown)
+    grad_acttwo, branch_term, owned_up, owned_down = lax.optimization_barrier(
+        (grad_acttwo, branch_term.astype(jnp.bfloat16), owned_up, owned_down)
+    )
+    grad_acttwo = grad_acttwo.astype(jnp.float32)
     branch_total = lax.psum(branch_term, "tp").astype(jnp.float32)
     output = (
         (residual + branch_total + down_bias)
@@ -420,7 +615,7 @@
         attn_cols,
         log_norm,
     )
-    key_value_totals = lax.psum_scatter(grad_kv, "ctx", scatter_dimension=0, tiled=False)
+    key_value_totals = kv_scatter(grad_kv)
     key_value_totals = key_value_totals.reshape(count_of_rows, 2 * shard_local_width)
     query_gradient_partial = grad_query.reshape(count_of_rows, shard_local_width)
     key_gradient_partial = key_value_totals[:, :shard_local_width]
@@ -428,22 +623,27 @@
     three = (query_gradient_partial, key_gradient_partial, value_gradient_partial)
     grad_qb = jnp.sum(query_gradient_partial.astype(jnp.float32), 0)
     grad_vb = jnp.sum(value_gradient_partial.astype(jnp.float32), 0)
-    grad_wqkv = jnp.stack(
-        [jnp.einsum("rd,rc->dc", act_one, part, preferred_element_type=jnp.float32) for part in three]
-    )
+    grad_three = [
+        jnp.einsum("rd,rc->dc", act_one, part, preferred_element_type=jnp.float32) for part in three
+    ]
     actone_term = sum(
         jnp.einsum("rc,dc->rd", part, wqkv_full[i], preferred_element_type=jnp.float32)
         for i, part in enumerate(three)
     )
     actone_term, output = lax.optimization_barrier((actone_term, output))
-    grad_actone = tp_total(actone_term)
+    grad_actone = lax.psum(actone_term.astype(jnp.bfloat16), "tp")
+    owned_qkv, owned_out = mixer_totals(grad_three, grad_wout)
+    grad_actone, owned_qkv, owned_out = lax.optimization_barrier(
+        (grad_actone, owned_qkv, owned_out)
+    )
+    grad_actone = grad_actone.astype(jnp.float32)
     input_norm = norm_back(grad_actone, unit_one, inv_one, ln1_gain)
     grad_g1 = jnp.sum(rows_part(grad_actone) * rows_part(unit_one), 0)
     grad_b1 = jnp.sum(rows_part(grad_actone), 0)
     grad_inputs = (
         (grad_resid + input_norm).astype(jnp.bfloat16).reshape(clip_count, block_len, model_width)
     )
-    owned = weight_totals(grad_wqkv, grad_wout, grad_wup, grad_wdown)
+    owned = (owned_qkv, owned_out, owned_up, owned_down)
     norm_rows_six = jnp.stack([grad_g1, grad_b1, grad_ob, grad_g2, grad_b2, grad_db])
     hidden_width = grad_ub.shape[0]
     if hidden_width == model_width and 2 * shard_local_width <= model_width:

time: 420 us -> 342 us (0.81)
  waiting for transfers between devices: 195 us -> 107 us
  Pallas kernels: 82.9 us -> 126 us
  blocking collectives: 19.7 us -> 0 us
  matrix products: 45 us -> 33.9 us
    psum x3 -> x1, waiting for transfers between devices: 116 us -> 52.7 us  [tp_total(): return lax.psum(values.astype(jnp.bfloat16), 'tp').astype(jnp.float32)]
    pallas_call x0 -> x3, Pallas kernels: none -> 47.5 us  [the longest x1 17.4 us: kv_scatter(): pl.pallas_call(kv_scatter_kernel, in_specs=[vmem], out_specs=vmem, out_sh...]
    psum x0 -> x2, waiting for transfers between devices: none -> 37.3 us  [the longest x1 18.7 us: shards(): grad_acttwo = lax.psum(acttwo_term.astype(jnp.bfloat16), 'tp')]
    reduce_scatter x1 -> x0, waiting for transfers between devices: 31.8 us -> none  [shards(): lax.psum_scatter(grad_kv, 'ctx', scatter_dimension=0, tiled=False)]
    all_gather x2 -> x0, blocking collectives: 19.7 us -> none  [the longest x1 13.8 us: shards(): lax.all_gather(w_qkv, 'shard', axis=1, tiled=True)]
    all_gather x1 -> x0, waiting for transfers between devices: 19.4 us -> none  [shards(): lax.all_gather(key_values.reshape(clip_count, block_len, 2 * shard_local_...]
    psum x1, waiting for transfers between devices: 26.8 us -> 16.2 us  [shards(): branch_total = lax.psum(branch_term, 'tp').astype(jnp.float32)]
    reshape x6 -> x0, local copies, waits for them, and re-layouts: 9.02 us -> none  [the longest x2 3.95 us: weight_totals(): down = low[3].reshape(2, hidden // 2, 2, half).transpose(0, 2, 1, 3)]
  transfers between devices with their start and end apart: 8 -> 6, of which waited for: 6 -> 4; matrix products, arithmetic and copies ran while one was open for 12% -> 14% of each run, Pallas kernels for 10% -> 22%
where the time goes in v2:
time: 342 us; the launch traced here: 341 us
  Pallas kernels  126 us (37%)
  waiting for transfers between devices  107 us (31%)
  matrix products  33.9 us (10%)
  other arithmetic  33.2 us (10%)
  local copies, waits for them, and re-layouts  24.4 us (7%)
  between operations  15.9 us (5%)
    psum x1, waiting for transfers between devices, tp_total(): return lax.psum(values.astype(jnp.bfloat16), 'tp').astype(jnp.float32)  52.7 us
    pallas_call x2, Pallas kernels, owner_sums(): pl.pallas_call(functools.partial(owner_sums_kernel, count), in_specs=[vme...  46.6 us
    psum x1, waiting for transfers between devices, shards(): grad_acttwo = lax.psum(acttwo_term.astype(jnp.bfloat16), 'tp')  18.7 us
    psum x1, waiting for transfers between devices, shards(): grad_actone = lax.psum(actone_term.astype(jnp.bfloat16), 'tp')  18.6 us
    pallas_call x1, Pallas kernels, kv_scatter(): pl.pallas_call(kv_scatter_kernel, in_specs=[vmem], out_specs=vmem, out_sh...  17.4 us
    pallas_call x1, Pallas kernels, kv_gather(): pl.pallas_call(kv_gather_kernel, in_specs=[vmem], out_specs=vmem, out_sha...  16.9 us
    psum x1, waiting for transfers between devices, shards(): branch_total = lax.psum(branch_term, 'tp').astype(jnp.float32)  16.2 us
    unnamed x98, local copies, waits for them, and re-layouts  14.4 us
  transfers between devices with their start and end apart: 6, of which 4 were waited for; matrix products, arithmetic and copies ran while one was open for 14% of the time, Pallas kernels for 22%

profile of v2, /device:TPU:0, one launch (start us, length us, event | category | flops | bytes accessed | tf_op | source)
XLA Modules:
  0.0 341.0 jit_solution(1158543749064533510)
XLA Ops:
  11.7 13.2 %shard_map.262 = (bf16[3,2,384,192]{3,2,1,0:T(8,128)(2,1)S(1)}, bf16[192,768]{1,0:T(8,128)(2,1)S(1)}) custom-call(bf16[3,384,192]{2,1,0:T(8,128)(2,1)S(1)} %copy.30.qkv_ref, bf16[192,384]{1,0:T(8,128)(2,1)S(1)} %copy-done.11), custom_call_target="tpu_custom_call" | custom-call | bytes 13271040 | tf_op jit(solution)/shard_map/pallas_call | solution.py:415
  30.6 16.9 %shard_map.263.kv_ref = bf16[4,2,384,384]{3,2,1,0:T(8,128)(2,1)S(1)} custom-call(bf16[2,384,384]{2,1,0:T(8,128)(2,1)S(1)} %pad_maximum_fusion.1.own_ref), custom_call_target="tpu_custom_call" | custom-call | bytes 23592960 | tf_op jit(solution)/shard_map/pallas_call | solution.py:300
  47.6 6.8 %shard_map.264 = (bf16[2,384,192]{2,1,0:T(8,128)(2,1)S(1)}, f32[2,192,384]{2,1,0:T(8,128)S(1)}, f32[2,8,384]{2,1,0:T(8,128)S(1)}) custom-call(bf16[2,384,192]{2,1,0:T(8,128)(2,1)S(1)} %add_convert_fusion.5.q_ref, bf16[4,2,384,384]{3,2,1,0:T(8,128)(2,1)S(1)} %shard_map.263.kv_ref), custom_call_target="tpu_custom_call" | custom-call | flops 905969664 | bytes 2949120 | tf_op jit(solution)/shard_map/pallas_call | solution.py:81
  61.8 52.7 %all-reduce.5.cloned.1.call-done = bf16[768,768]{1,0:T(8,128)(2,1)} async-done(((bf16[768,768]{1,0:T(8,128)(2,1)}), bf16[768,768]{1,0:T(8,128)(2,1)}) %all-reduce.5.cloned.1.call-update) | async-done | bytes 1179664 | tf_op jit(solution)/shard_map/psum | solution.py:495
  116.3 2.4 fusion.16
  120.6 8.6 %fusion.8 = (bf16[768,768]{1,0:T(8,128)(2,1)}, f32[768,768]{1,0:T(8,128)}) fusion(f32[768]{0:T(1024)S(1)} %copy-done.42, bf16[768,768]{1,0:T(8,128)(2,1)} %all-gather.5.cloned.1.call-done, f32[768,768]{1,0:T(8,128)} %subtract_multiply_fusion, f32[768]{0:T(1024)S(1)} %copy-done.43, f32[768]{0:T(1024)S(1)} %copy-done.36), kind=kOutput, calls=%fused_computation.10 | convolution fusion | flops 946667520 | bytes 7087104 | tf_op jit(solution)/shard_map/dot_general | solution.py:578
  129.2 3.5 %convert_reduce_fusion.1 = (f32[768]{0:T(1024)S(1)}, bf16[768,768]{1,0:T(8,128)(2,1)S(1)}) fusion(f32[768,768]{1,0:T(8,128)} %get-tuple-element.84, f32[768]{0:T(1024)S(1)} %copy-done.42, bf16[768,768]{1,0:T(8,128)(2,1)S(1)} %bitcast.101, bf16[768,768]{1,0:T(8,128)(2,1)} %all-gather.3.cloned.1.call-done), kind=kOutput, calls=%fused_computation.23 | convolution fusion | flops 913636608 | bytes 5904384 | tf_op jit(solution)/shard_map/rd,fd->rf/dot_general | solution.py:585
  133.8 2.1 convolution_convert_fusion.3
  137.7 2.1 convolution_convert_fusion
  141.0 28.7 %shard_map.265 = (f32[2,192,768]{2,1,0:T(8,128)S(1)}, f32[2,384,384]{2,1,0:T(8,128)S(1)}) custom-call(bf16[2,2,192,768]{3,2,1,0:T(8,128)(2,1)S(1)} %bitcast.95, bf16[2,384,768]{2,1,0:T(8,128)(2,1)} %bitcast.111), custom_call_target="tpu_custom_call" | custom-call | flops 1179648 | bytes 35389440 | tf_op jit(solution)/shard_map/pallas_call | solution.py:261
  172.9 18.7 %all-reduce.7.cloned.1.call-done = bf16[768,768]{1,0:T(8,128)(2,1)} async-done(((bf16[768,768]{1,0:T(8,128)(2,1)}), bf16[768,768]{1,0:T(8,128)(2,1)}) %all-reduce.7.cloned.1.call-update) | async-done | bytes 1179664 | tf_op jit(solution)/shard_map/psum | solution.py:590
  191.9 2.7 multiply_reduce_fusion.4
  198.3 11.9 %shard_map.266 = (bf16[2,384,192]{2,1,0:T(8,128)(2,1)S(1)}, bf16[4,2,384,384]{3,2,1,0:T(8,128)(2,1)}) custom-call(bf16[2,384,192]{2,1,0:T(8,128)(2,1)S(1)} %add_convert_fusion.5.q_ref, bf16[4,2,384,384]{3,2,1,0:T(8,128)(2,1)} %copy-done, bf16[2,384,192]{2,1,0:T(8,128)(2,1)S(1)} %bitcast.98, f32[2,192,384]{2,1,0:T(8,128)S(1)} %copy-done.13, ...), custom_call_target="tpu_custom_call" | custom-call | flops 2264924160 | bytes 5898240 | tf_op jit(solution)/shard_map/pallas_call | solution.py:133
  213.0 17.4 %shard_map.267 = bf16[2,384,384]{2,1,0:T(8,128)(2,1)S(1)} custom-call(bf16[4,2,384,384]{3,2,1,0:T(8,128)(2,1)S(1)} %copy-done.1), custom_call_target="tpu_custom_call" | custom-call | bytes 29491200 | tf_op jit(solution)/shard_map/pallas_call | solution.py:347
  233.8 16.2 %all-reduce.9.cloned.1.call-done = bf16[768,768]{1,0:T(8,128)(2,1)} async-done(((bf16[768,768]{1,0:T(8,128)(2,1)}), bf16[768,768]{1,0:T(8,128)(2,1)}) %all-reduce.9.cloned.1.call-update) | async-done | bytes 1179664 | tf_op jit(solution)/shard_map/psum | solution.py:596
  250.0 3.3 add_convert_fusion.2
  258.5 2.3 convolution_convert_fusion.6
  261.0 2.8 convolution_convert_fusion.7
  265.0 2.1 convolution_convert_fusion.5
  267.2 17.9 %shard_map.268 = (f32[2,192,192]{2,1,0:T(8,128)S(1)}, f32[2,192,192]{2,1,0:T(8,128)S(1)}, f32[2,192,192]{2,1,0:T(8,128)S(1)}, f32[2,96,384]{2,1,0:T(8,128)S(1)}) custom-call(bf16[2,2,192,192]{3,2,1,0:T(8,128)(2,1)S(1)} %bitcast.88, bf16[2,2,192,192]{3,2,1,0:T(8,128)(2,1)S(1)} %bitcast.90, bf16[2,2,192,192]{3,2,1,0:T(8,128)(2,1)S(1)} %bitcast.89, ...), custom_call_target="tpu_custom_call" | custom-call | flops 589824 | bytes 17694720 | tf_op jit(solution)/shard_map/pallas_call | solution.py:261
  290.4 18.6 %all-reduce.11.cloned.1.call-done = bf16[768,768]{1,0:T(8,128)(2,1)} async-done(((bf16[768,768]{1,0:T(8,128)(2,1)}), bf16[768,768]{1,0:T(8,128)(2,1)}) %all-reduce.11.cloned.1.call-update) | async-done | bytes 1179664 | tf_op jit(solution)/shard_map/psum | solution.py:634
  311.8 2.3 multiply_reduce_fusion.3
  314.2 12.6 %shard_map.269 = f32[16,768]{1,0:T(8,128)S(1)} custom-call(f32[16,768]{1,0:T(8,128)S(1)} %concatenate.12.vec_ref), custom_call_target="tpu_custom_call" | custom-call | flops 12288 | bytes 491520 | tf_op jit(solution)/shard_map/pallas_call | solution.py:475
  328.1 3.0 add_convert_fusion
  (177 shorter events, 56.0 us)
Async XLA Ops:
  8.0 17.0 %copy-start.14 = (bf16[2,384,768]{2,1,0:T(8,128)(2,1)S(1)}, bf16[2,384,768]{2,1,0:T(8,128)(2,1)}, u32[]{:S(2)}) copy-start(bf16[2,384,768]{2,1,0:T(8,128)(2,1)} %param.15) | copy-start | bytes 3538948
  8.0 3.7 %copy-start.11 = (bf16[192,384]{1,0:T(8,128)(2,1)S(1)}, bf16[192,384]{1,0:T(8,128)(2,1)}, u32[]{:S(2)}) copy-start(bf16[192,384]{1,0:T(8,128)(2,1)} %out_ref.1) | copy-start | bytes 442372
  8.0 16.9 %copy-start.33 = (f32[768]{0:T(1024)S(1)}, f32[768]{0:T(1024)}, u32[]{:S(2)}) copy-start(f32[768]{0:T(1024)} %param.17) | copy-start | bytes 9220
  8.1 16.9 %copy-start.35 = (f32[768]{0:T(1024)S(1)}, f32[768]{0:T(1024)}, u32[]{:S(2)}) copy-start(f32[768]{0:T(1024)} %param.18) | copy-start | bytes 9220
  8.1 106.4 %all-reduce.5.cloned.1.call-start = ((), (), s32[]{:S(2)}) async-start(), calls=%async_computation | async-start | bytes 2359296 | tf_op jit(solution)/shard_map/psum | solution.py:495
  26.8 3.5 %copy-start.38 = (f32[192]{0:T(256)S(1)}, f32[192]{0:T(256)}, u32[]{:S(2)}) copy-start(f32[192]{0:T(256)} %param.21) | copy-start | bytes 2308
  30.4 17.2 %copy-start.39 = (f32[192]{0:T(256)S(1)}, f32[192]{0:T(256)}, u32[]{:S(2)}) copy-start(f32[192]{0:T(256)} %param.20) | copy-start | bytes 2308
  47.5 6.9 %copy-start = (bf16[4,2,384,384]{3,2,1,0:T(8,128)(2,1)}, bf16[4,2,384,384]{3,2,1,0:T(8,128)(2,1)S(1)}, u32[]{:S(2)}) copy-start(bf16[4,2,384,384]{3,2,1,0:T(8,128)(2,1)S(1)} %shard_map.263.kv_ref) | copy-start | bytes 7077892
  55.3 3.7 %copy-start.24 = (bf16[2,384,768]{2,1,0:T(8,128)(2,1)S(1)}, bf16[2,384,768]{2,1,0:T(8,128)(2,1)}, u32[]{:S(2)}) copy-start(bf16[2,384,768]{2,1,0:T(8,128)(2,1)} %param.16) | copy-start | bytes 3538948
  57.5 63.1 %all-gather.5.cloned.1.call-start = ((), (), s32[]{:S(2)}) async-start(), calls=%async_computation.2 | async-start | bytes 1769472 | tf_op jit(solution)/shard_map/all_gather | solution.py:556
  58.1 56.3 %copy-start.34 = (f32[768]{0:T(1024)S(1)}, f32[768]{0:T(1024)}, u32[]{:S(2)}) copy-start(f32[768]{0:T(1024)} %param.23) | copy-start | bytes 9220
  58.1 71.1 %all-gather.3.cloned.1.call-start = ((), (), s32[]{:S(2)}) async-start(), calls=%async_computation.1 | async-start | bytes 1769472 | tf_op jit(solution)/shard_map/all_gather | solution.py:557
  58.7 132.8 %all-reduce.7.cloned.1.call-start = ((), (), s32[]{:S(2)}) async-start(), calls=%async_computation.3 | async-start | bytes 2359296 | tf_op jit(solution)/shard_map/psum | solution.py:590
  129.2 4.6 %copy-start.41 = (bf16[768,768]{1,0:T(8,128)(2,1)S(1)}, bf16[768,768]{1,0:T(8,128)(2,1)}, u32[]{:S(2)}) copy-start(bf16[768,768]{1,0:T(8,128)(2,1)} %all-gather.5.cloned.1.call-done) | copy-start | bytes 3538948
  136.0 114.1 %all-reduce.9.cloned.1.call-start = ((), (), s32[]{:S(2)}) async-start(), calls=%async_computation.4 | async-start | bytes 2359296 | tf_op jit(solution)/shard_map/psum | solution.py:596
  141.0 29.8 %copy-start.40 = (bf16[768,768]{1,0:T(8,128)(2,1)S(1)}, bf16[768,768]{1,0:T(8,128)(2,1)}, u32[]{:S(2)}) copy-start(bf16[768,768]{1,0:T(8,128)(2,1)} %all-gather.3.cloned.1.call-done) | copy-start | bytes 3538948
  191.6 117.4 %all-reduce.11.cloned.1.call-start = ((), (), s32[]{:S(2)}) async-start(), calls=%async_computation.5 | async-start | bytes 2359296 | tf_op jit(solution)/shard_map/psum | solution.py:634
  198.3 11.9 %copy-start.27 = (bf16[2,384,768]{2,1,0:T(8,128)(2,1)S(1)}, bf16[2,384,768]{2,1,0:T(8,128)(2,1)}, u32[]{:S(2)}) copy-start(bf16[2,384,768]{2,1,0:T(8,128)(2,1)} %copy-done.26) | copy-start | bytes 3538948
  210.2 20.4 %copy-start.30 = (bf16[1,2,384,192]{3,2,1,0:T(8,128)(2,1)S(1)}, bf16[1,2,384,192]{3,2,1,0:T(8,128)(2,1)}, u32[]{:S(2)}) copy-start(bf16[1,2,384,192]{3,2,1,0:T(8,128)(2,1)} %get-tuple-element.79) | copy-start | bytes 884740
  232.2 17.8 %copy-start.15 = (bf16[2,384,768]{2,1,0:T(8,128)(2,1)S(1)}, bf16[2,384,768]{2,1,0:T(8,128)(2,1)}, u32[]{:S(2)}) copy-start(bf16[2,384,768]{2,1,0:T(8,128)(2,1)} %param.15) | copy-start | bytes 3538948
  232.2 17.8 %copy-start.37 = (f32[768]{0:T(1024)S(1)}, f32[768]{0:T(1024)}, u32[]{:S(2)}) copy-start(f32[768]{0:T(1024)} %param.29) | copy-start | bytes 9220
  260.9 4.2 %copy-start.3 = (bf16[2,384,192]{2,1,0:T(8,128)(2,1)S(1)}, bf16[2,384,192]{2,1,0:T(8,128)(2,1)}, u32[]{:S(2)}) copy-start(bf16[2,384,192]{2,1,0:T(8,128)(2,1)} %copy-done.2) | copy-start | bytes 884740
  311.8 16.3 %copy-start.18 = (f32[768,768]{1,0:T(8,128)S(1)}, f32[768,768]{1,0:T(8,128)}, u32[]{:S(2)}) copy-start(f32[768,768]{1,0:T(8,128)} %copy-done.17) | copy-start | bytes 7077892
  328.1 3.7 %copy-start.5 = (f32[2,192,768]{2,1,0:T(8,128)S(1)}, f32[2,192,768]{2,1,0:T(8,128)}, u32[]{:S(2)}) copy-start(f32[2,192,768]{2,1,0:T(8,128)} %copy-done.4) | copy-start | bytes 3538948
  (29 other events, 51.3 us)
Sparse Core Ops, SparseCore 0:
  57.7 56.7 all-reduce.4
  136.1 55.4 all-reduce.6
  194.5 55.4 all-reduce.8
  253.4 55.5 all-reduce.10
Sparse Core Ops, SparseCore 1:
  59.5 23.4 all-gather.4
  84.5 22.7 all-gather.2

commit v3 on v2

--- a/solution.py
+++ b/solution.py
@@ -456,7 +456,8 @@
         remote(line_out, line_in.at[step], (sems_b.at[0], sems_b.at[1]), step, lines[step])
         for step in range(n_tp - 1)
     ]
-    out_ref[rows_all:] = total[rows_all:]
+    if rows_all < vec_ref.shape[0]:
+        out_ref[rows_all:] = total[rows_all:]
     for copy in copies:
         copy.wait()
     total = jnp.zeros_like(line_out[...])
@@ -467,7 +468,7 @@
     out_ref[:rows_all] = total
 
 
-def small_sums(vec, rows_all):
+def small_sums(vec, rows_all, collective):
     plane = lax.axis_size("shard") * lax.axis_size("ctx")
     n_tp = lax.axis_size("tp")
     vmem = pl.BlockSpec(memory_space=pltpu.VMEM)
@@ -485,7 +486,7 @@
             pltpu.SemaphoreType.DMA((2, n_tp - 1)),
         ],
         compiler_params=pltpu.CompilerParams(
-            collective_id=7, has_side_effects=True, vmem_limit_bytes=VMEM_BYTES
+            collective_id=collective, has_side_effects=True, vmem_limit_bytes=VMEM_BYTES
         ),
         cost_estimate=pl.CostEstimate(flops=vec.size, bytes_accessed=vec.size * 40, transcendentals=0),
     )(vec)
@@ -524,6 +525,31 @@
     )
     qkv = jnp.stack([g.reshape(width // 2, local) for g in sums[:3]])
     return qkv, sums[3].reshape(local, width // 2)
+
+
+def late_sums(rows):
+    if not in_pairs():
+        return lax.psum(rows, ("shard", "ctx", "tp"))
+    return small_sums(rows, rows.shape[0], 7)
+
+
+def early_sums(rows, vectors):
+    q_vec, v_vec, up_vec = vectors
+    model_width, local = rows.shape[1], q_vec.shape[0]
+    if not in_pairs() or up_vec.shape[0] != model_width or 2 * local > model_width:
+        return lax.psum(rows, ("shard", "ctx", "tp")), lax.psum(vectors, ("shard", "ctx"))
+    pad = jnp.zeros((model_width - 2 * local,), jnp.float32)
+    packed = jnp.concatenate(
+        [
+            rows,
+            jnp.zeros((4, model_width), jnp.float32),
+            up_vec[None],
+            jnp.concatenate([q_vec, v_vec, pad])[None],
+            jnp.zeros((6, model_width), jnp.float32),
+        ]
+    )
+    summed = small_sums(packed, 8, 11)
+    return summed[:4], (summed[9, :local], summed[9, local : 2 * local], summed[8])
 
 
 def shards(
@@ -593,12 +619,7 @@
         (grad_acttwo, branch_term.astype(jnp.bfloat16), owned_up, owned_down)
     )
     grad_acttwo = grad_acttwo.astype(jnp.float32)
-    branch_total = lax.psum(branch_term, "tp").astype(jnp.float32)
-    output = (
-        (residual + branch_total + down_bias)
-        .astype(jnp.bfloat16)
-        .reshape(clip_count, block_len, model_width)
-    )
+    branch_low = lax.psum(branch_term, "tp")
     grad_resid = grad_y + norm_back(grad_acttwo, unit_two, inv_two, ln2_gain)
     grad_g2 = jnp.sum(rows_part(grad_acttwo) * rows_part(unit_two), 0)
     grad_b2 = jnp.sum(rows_part(grad_acttwo), 0)
@@ -630,11 +651,20 @@
         jnp.einsum("rc,dc->rd", part, wqkv_full[i], preferred_element_type=jnp.float32)
         for i, part in enumerate(three)
     )
-    actone_term, output = lax.optimization_barrier((actone_term, output))
-    grad_actone = lax.psum(actone_term.astype(jnp.bfloat16), "tp")
+    actone_term, branch_low = lax.optimization_barrier((actone_term.astype(jnp.bfloat16), branch_low))
+    branch_total = branch_low.astype(jnp.float32)
+    output = (
+        (residual + branch_total + down_bias)
+        .astype(jnp.bfloat16)
+        .reshape(clip_count, block_len, model_width)
+    )
+    grad_actone = lax.psum(actone_term, "tp")
     owned_qkv, owned_out = mixer_totals(grad_three, grad_wout)
-    grad_actone, owned_qkv, owned_out = lax.optimization_barrier(
-        (grad_actone, owned_qkv, owned_out)
+    early, vectors = early_sums(
+        jnp.stack([grad_ob, grad_g2, grad_b2, grad_db]), (grad_qb, grad_vb, grad_ub)
+    )
+    grad_actone, owned_qkv, owned_out, early = lax.optimization_barrier(
+        (grad_actone, owned_qkv, owned_out, early)
     )
     grad_actone = grad_actone.astype(jnp.float32)
     input_norm = norm_back(grad_actone, unit_one, inv_one, ln1_gain)
@@ -644,29 +674,7 @@
         (grad_resid + input_norm).astype(jnp.bfloat16).reshape(clip_count, block_len, model_width)
     )
     owned = (owned_qkv, owned_out, owned_up, owned_down)
-    norm_rows_six = jnp.stack([grad_g1, grad_b1, grad_ob, grad_g2, grad_b2, grad_db])
-    hidden_width = grad_ub.shape[0]
-    if hidden_width == model_width and 2 * shard_local_width <= model_width:
-        pad = jnp.zeros((model_width - 2 * shard_local_width,), jnp.float32)
-        packed = jnp.concatenate(
-            [
-                norm_rows_six,
-                jnp.zeros((2, model_width), jnp.float32),
-                grad_ub[None],
-                jnp.concatenate([grad_qb, grad_vb, pad])[None],
-                jnp.zeros((6, model_width), jnp.float32),
-            ]
-        )
-        summed = small_sums(packed, 8)
-        norm_sums = summed[:6]
-        vectors = (
-            summed[9, :shard_local_width],
-            summed[9, shard_local_width : 2 * shard_local_width],
-            summed[8],
-        )
-    else:
-        vectors = lax.psum((grad_qb, grad_vb, grad_ub), ("shard", "ctx"))
-        norm_sums = lax.psum(norm_rows_six, ("shard", "ctx", "tp"))
+    norm_sums = (*late_sums(jnp.stack([grad_g1, grad_b1])), *early)
     return (
         output,
         grad_inputs,

time: 342 us -> 343 us (level)
  Pallas kernels: 126 us -> 136 us
  other arithmetic: 33.2 us -> 28.7 us
  local copies, waits for them, and re-layouts: 24.4 us -> 20.8 us
    pallas_call x1 -> x2, Pallas kernels: 12.6 us -> 23.5 us  [small_sums(): pl.pallas_call(functools.partial(small_sums_kernel, rows_all), in_specs=[...]
    unnamed x98 -> x104, local copies, waits for them, and re-layouts: 14.4 us -> 12.3 us
  transfers between devices with their start and end apart: 6 -> 6, of which waited for: 4 -> 4; matrix products, arithmetic and copies ran while one was open for 14% -> 12% of each run, Pallas kernels for 22% -> 26%
where the time goes in v3:
time: 343 us; the launch traced here: 342 us
  Pallas kernels  136 us (40%)
  waiting for transfers between devices  106 us (31%)
  matrix products  33.7 us (10%)
  other arithmetic  28.7 us (8%)
  local copies, waits for them, and re-layouts  20.8 us (6%)
  between operations  16.1 us (5%)
    psum x1, waiting for transfers between devices, tp_total(): return lax.psum(values.astype(jnp.bfloat16), 'tp').astype(jnp.float32)  52.1 us
    pallas_call x2, Pallas kernels, owner_sums(): pl.pallas_call(functools.partial(owner_sums_kernel, count), in_specs=[vme...  46.9 us
    pallas_call x2, Pallas kernels, small_sums(): pl.pallas_call(functools.partial(small_sums_kernel, rows_all), in_specs=[...  23.5 us
    psum x1, waiting for transfers between devices, shards(): grad_acttwo = lax.psum(acttwo_term.astype(jnp.bfloat16), 'tp')  18.5 us
    pallas_call x1, Pallas kernels, kv_scatter(): pl.pallas_call(kv_scatter_kernel, in_specs=[vmem], out_specs=vmem, out_sh...  17.4 us
    psum x1, waiting for transfers between devices, shards(): branch_low = lax.psum(branch_term, 'tp')  17.2 us
    pallas_call x1, Pallas kernels, kv_gather(): pl.pallas_call(kv_gather_kernel, in_specs=[vmem], out_specs=vmem, out_sha...  16.9 us
    psum x1, waiting for transfers between devices, shards(): grad_actone = lax.psum(actone_term, 'tp')  16.7 us
  transfers between devices with their start and end apart: 6, of which 4 were waited for; matrix products, arithmetic and copies ran while one was open for 12% of the time, Pallas kernels for 26%

profile of v3, /device:TPU:0, one launch (start us, length us, event | category | flops | bytes accessed | tf_op | source)
XLA Modules:
  0.0 342.0 jit_solution(13783006146297130567)
XLA Ops:
  11.7 13.2 %shard_map.262 = (bf16[3,2,384,192]{3,2,1,0:T(8,128)(2,1)S(1)}, bf16[192,768]{1,0:T(8,128)(2,1)S(1)}) custom-call(bf16[3,384,192]{2,1,0:T(8,128)(2,1)S(1)} %copy.30.qkv_ref, bf16[192,384]{1,0:T(8,128)(2,1)S(1)} %copy-done.11), custom_call_target="tpu_custom_call" | custom-call | bytes 13271040 | tf_op jit(solution)/shard_map/pallas_call | solution.py:415
  28.8 16.9 %shard_map.263.kv_ref = bf16[4,2,384,384]{3,2,1,0:T(8,128)(2,1)S(1)} custom-call(bf16[2,384,384]{2,1,0:T(8,128)(2,1)S(1)} %pad_maximum_fusion.1.own_ref), custom_call_target="tpu_custom_call" | custom-call | bytes 23592960 | tf_op jit(solution)/shard_map/pallas_call | solution.py:300
  45.9 6.8 %shard_map.264 = (bf16[2,384,192]{2,1,0:T(8,128)(2,1)S(1)}, f32[2,192,384]{2,1,0:T(8,128)S(1)}, f32[2,8,384]{2,1,0:T(8,128)S(1)}) custom-call(bf16[2,384,192]{2,1,0:T(8,128)(2,1)S(1)} %add_convert_fusion.6.q_ref, bf16[4,2,384,384]{3,2,1,0:T(8,128)(2,1)S(1)} %shard_map.263.kv_ref), custom_call_target="tpu_custom_call" | custom-call | flops 905969664 | bytes 2949120 | tf_op jit(solution)/shard_map/pallas_call | solution.py:81
  60.5 52.1 %all-reduce.5.cloned.1.call-done = bf16[768,768]{1,0:T(8,128)(2,1)} async-done(((bf16[768,768]{1,0:T(8,128)(2,1)}), bf16[768,768]{1,0:T(8,128)(2,1)}) %all-reduce.5.cloned.1.call-update) | async-done | bytes 1179664 | tf_op jit(solution)/shard_map/psum | solution.py:496
  114.5 2.4 fusion.16
  118.8 8.6 %fusion.8 = (bf16[768,768]{1,0:T(8,128)(2,1)}, f32[768,768]{1,0:T(8,128)}) fusion(f32[768]{0:T(1024)S(1)} %copy-done.45, bf16[768,768]{1,0:T(8,128)(2,1)} %all-gather.5.cloned.1.call-done, f32[768,768]{1,0:T(8,128)} %subtract_multiply_fusion, f32[768]{0:T(1024)S(1)} %copy-done.46, f32[768]{0:T(1024)S(1)} %copy-done.38), kind=kOutput, calls=%fused_computation.10 | convolution fusion | flops 946667520 | bytes 7087104 | tf_op jit(solution)/shard_map/dot_general | solution.py:604
  127.4 3.4 %convert_reduce_fusion.1 = (f32[768]{0:T(1024)S(1)}, bf16[768,768]{1,0:T(8,128)(2,1)S(1)}) fusion(f32[768,768]{1,0:T(8,128)} %get-tuple-element.87, f32[768]{0:T(1024)S(1)} %copy-done.45, bf16[768,768]{1,0:T(8,128)(2,1)S(1)} %bitcast.101, bf16[768,768]{1,0:T(8,128)(2,1)} %all-gather.3.cloned.1.call-done), kind=kOutput, calls=%fused_computation.25 | convolution fusion | flops 913636608 | bytes 5904384 | tf_op jit(solution)/shard_map/rd,fd->rf/dot_general | solution.py:611
  132.0 2.1 convolution_convert_fusion.3
  136.2 2.1 convolution_convert_fusion
  139.4 28.7 %shard_map.265 = (f32[2,192,768]{2,1,0:T(8,128)S(1)}, f32[2,384,384]{2,1,0:T(8,128)S(1)}) custom-call(bf16[2,2,192,768]{3,2,1,0:T(8,128)(2,1)S(1)} %bitcast.95, bf16[2,384,768]{2,1,0:T(8,128)(2,1)} %bitcast.112), custom_call_target="tpu_custom_call" | custom-call | flops 1179648 | bytes 35389440 | tf_op jit(solution)/shard_map/pallas_call | solution.py:261
  171.3 18.5 %all-reduce.7.cloned.1.call-done = bf16[768,768]{1,0:T(8,128)(2,1)} async-done(((bf16[768,768]{1,0:T(8,128)(2,1)}), bf16[768,768]{1,0:T(8,128)(2,1)}) %all-reduce.7.cloned.1.call-update) | async-done | bytes 1179664 | tf_op jit(solution)/shard_map/psum | solution.py:616
  189.8 2.7 multiply_reduce_fusion.4
  198.1 11.7 %shard_map.266 = (bf16[2,384,192]{2,1,0:T(8,128)(2,1)S(1)}, bf16[4,2,384,384]{3,2,1,0:T(8,128)(2,1)}) custom-call(bf16[2,384,192]{2,1,0:T(8,128)(2,1)S(1)} %add_convert_fusion.6.q_ref, bf16[4,2,384,384]{3,2,1,0:T(8,128)(2,1)} %copy-done, bf16[2,384,192]{2,1,0:T(8,128)(2,1)S(1)} %bitcast.98, f32[2,192,384]{2,1,0:T(8,128)S(1)} %copy-done.14, ...), custom_call_target="tpu_custom_call" | custom-call | flops 2264924160 | bytes 5898240 | tf_op jit(solution)/shard_map/pallas_call | solution.py:133
  211.5 17.4 %shard_map.267 = bf16[2,384,384]{2,1,0:T(8,128)(2,1)S(1)} custom-call(bf16[4,2,384,384]{3,2,1,0:T(8,128)(2,1)S(1)} %copy-done.1), custom_call_target="tpu_custom_call" | custom-call | bytes 29491200 | tf_op jit(solution)/shard_map/pallas_call | solution.py:347
  230.8 2.4 convolution_convert_fusion.6
  236.3 17.2 %all-reduce.9.cloned.1.call-done = bf16[768,768]{1,0:T(8,128)(2,1)} async-done(((bf16[768,768]{1,0:T(8,128)(2,1)}), bf16[768,768]{1,0:T(8,128)(2,1)}) %all-reduce.9.cloned.1.call-update) | async-done | bytes 1179664 | tf_op jit(solution)/shard_map/psum | solution.py:622
  255.3 13.7 %shard_map.269 = f32[16,768]{1,0:T(8,128)S(1)} custom-call(f32[16,768]{1,0:T(8,128)S(1)} %concatenate.12.vec_ref), custom_call_target="tpu_custom_call" | custom-call | flops 12288 | bytes 491520 | tf_op jit(solution)/shard_map/pallas_call | solution.py:476
  269.4 2.1 convolution_convert_fusion.7
  271.7 2.1 convolution_convert_fusion.5
  273.8 18.2 %shard_map.268 = (f32[2,192,192]{2,1,0:T(8,128)S(1)}, f32[2,192,192]{2,1,0:T(8,128)S(1)}, f32[2,192,192]{2,1,0:T(8,128)S(1)}, f32[2,96,384]{2,1,0:T(8,128)S(1)}) custom-call(bf16[2,2,192,192]{3,2,1,0:T(8,128)(2,1)S(1)} %bitcast.88, bf16[2,2,192,192]{3,2,1,0:T(8,128)(2,1)S(1)} %bitcast.90, bf16[2,2,192,192]{3,2,1,0:T(8,128)(2,1)S(1)} %bitcast.89, ...), custom_call_target="tpu_custom_call" | custom-call | flops 589824 | bytes 17694720 | tf_op jit(solution)/shard_map/pallas_call | solution.py:261
  297.2 16.7 %all-reduce.11.cloned.1.call-done = bf16[768,768]{1,0:T(8,128)(2,1)} async-done(((bf16[768,768]{1,0:T(8,128)(2,1)}), bf16[768,768]{1,0:T(8,128)(2,1)}) %all-reduce.11.cloned.1.call-update) | async-done | bytes 1179664 | tf_op jit(solution)/shard_map/psum | solution.py:661
  313.8 2.7 multiply_reduce_fusion.3
  319.2 9.8 %shard_map.270 = f32[2,768]{1,0:T(2,128)S(1)} custom-call(f32[2,768]{1,0:T(2,128)S(1)} %pad_maximum_fusion.2.vec_ref), custom_call_target="tpu_custom_call" | custom-call | flops 1536 | bytes 61440 | tf_op jit(solution)/shard_map/pallas_call | solution.py:476
  329.7 2.5 add_convert_fusion
  (188 shorter events, 51.8 us)
Async XLA Ops:
  8.0 17.0 %copy-start.15 = (bf16[2,384,768]{2,1,0:T(8,128)(2,1)S(1)}, bf16[2,384,768]{2,1,0:T(8,128)(2,1)}, u32[]{:S(2)}) copy-start(bf16[2,384,768]{2,1,0:T(8,128)(2,1)} %param.15) | copy-start | bytes 3538948
  8.0 16.9 %copy-start.34 = (f32[768]{0:T(1024)S(1)}, f32[768]{0:T(1024)}, u32[]{:S(2)}) copy-start(f32[768]{0:T(1024)} %param.17) | copy-start | bytes 9220
  8.1 16.9 %copy-start.36 = (f32[768]{0:T(1024)S(1)}, f32[768]{0:T(1024)}, u32[]{:S(2)}) copy-start(f32[768]{0:T(1024)} %param.18) | copy-start | bytes 9220
  8.1 104.6 %all-reduce.5.cloned.1.call-start = ((), (), s32[]{:S(2)}) async-start(), calls=%async_computation | async-start | bytes 2359296 | tf_op jit(solution)/shard_map/psum | solution.py:496
  28.6 17.2 %copy-start.28 = (f32[1,768,192]{2,1,0:T(8,128)S(1)}, f32[1,768,192]{2,1,0:T(8,128)}, u32[]{:S(2)}) copy-start(f32[1,768,192]{2,1,0:T(8,128)} %copy.32) | copy-start | bytes 1769476
  28.6 17.2 %copy-start.42 = (f32[192]{0:T(256)S(1)}, f32[192]{0:T(256)}, u32[]{:S(2)}) copy-start(f32[192]{0:T(256)} %param.20) | copy-start | bytes 2308
  45.7 6.9 %copy-start = (bf16[4,2,384,384]{3,2,1,0:T(8,128)(2,1)}, bf16[4,2,384,384]{3,2,1,0:T(8,128)(2,1)S(1)}, u32[]{:S(2)}) copy-start(bf16[4,2,384,384]{3,2,1,0:T(8,128)(2,1)S(1)} %shard_map.263.kv_ref) | copy-start | bytes 7077892
  55.7 63.1 %all-gather.5.cloned.1.call-start = ((), (), s32[]{:S(2)}) async-start(), calls=%async_computation.2 | async-start | bytes 1769472 | tf_op jit(solution)/shard_map/all_gather | solution.py:582
  56.3 56.3 %copy-start.16 = (bf16[2,384,768]{2,1,0:T(8,128)(2,1)S(1)}, bf16[2,384,768]{2,1,0:T(8,128)(2,1)}, u32[]{:S(2)}) copy-start(bf16[2,384,768]{2,1,0:T(8,128)(2,1)} %param.15) | copy-start | bytes 3538948
  56.3 56.3 %copy-start.35 = (f32[768]{0:T(1024)S(1)}, f32[768]{0:T(1024)}, u32[]{:S(2)}) copy-start(f32[768]{0:T(1024)} %param.23) | copy-start | bytes 9220
  56.3 71.1 %all-gather.3.cloned.1.call-start = ((), (), s32[]{:S(2)}) async-start(), calls=%async_computation.1 | async-start | bytes 1769472 | tf_op jit(solution)/shard_map/all_gather | solution.py:583
  56.9 132.9 %all-reduce.7.cloned.1.call-start = ((), (), s32[]{:S(2)}) async-start(), calls=%async_computation.3 | async-start | bytes 2359296 | tf_op jit(solution)/shard_map/psum | solution.py:616
  127.4 4.6 %copy-start.44 = (bf16[768,768]{1,0:T(8,128)(2,1)S(1)}, bf16[768,768]{1,0:T(8,128)(2,1)}, u32[]{:S(2)}) copy-start(bf16[768,768]{1,0:T(8,128)(2,1)} %all-gather.5.cloned.1.call-done) | copy-start | bytes 3538948
  134.2 119.4 %all-reduce.9.cloned.1.call-start = ((), (), s32[]{:S(2)}) async-start(), calls=%async_computation.4 | async-start | bytes 2359296 | tf_op jit(solution)/shard_map/psum | solution.py:622
  139.4 29.8 %copy-start.43 = (bf16[768,768]{1,0:T(8,128)(2,1)S(1)}, bf16[768,768]{1,0:T(8,128)(2,1)}, u32[]{:S(2)}) copy-start(bf16[768,768]{1,0:T(8,128)(2,1)} %all-gather.3.cloned.1.call-done) | copy-start | bytes 3538948
  197.9 116.0 %all-reduce.11.cloned.1.call-start = ((), (), s32[]{:S(2)}) async-start(), calls=%async_computation.5 | async-start | bytes 2359296 | tf_op jit(solution)/shard_map/psum | solution.py:661
  211.5 19.2 %copy-start.39 = (f32[1,768]{1,0:T(1,128)S(1)}, f32[1,768]{1,0:T(1,128)}, u32[]{:S(2)}) copy-start(f32[1,768]{1,0:T(1,128)} %stack.28) | copy-start | bytes 9220
  211.5 19.3 %copy-start.37 = (f32[768]{0:T(1024)S(1)}, f32[768]{0:T(1024)}, u32[]{:S(2)}) copy-start(f32[768]{0:T(1024)} %param.18) | copy-start | bytes 9220
  269.0 27.6 %copy-start.12 = (f32[16,768]{1,0:T(8,128)}, f32[16,768]{1,0:T(8,128)S(1)}, u32[]{:S(2)}) copy-start(f32[16,768]{1,0:T(8,128)S(1)} %shard_map.269) | copy-start | bytes 147460
  313.8 15.8 %copy-start.32 = (bf16[768,768]{1,0:T(8,128)(2,1)S(1)}, bf16[768,768]{1,0:T(8,128)(2,1)}, u32[]{:S(2)}) copy-start(bf16[768,768]{1,0:T(8,128)(2,1)} %all-reduce.9.cloned.1.call-done) | copy-start | bytes 3538948
  316.5 13.1 %copy-start.17 = (bf16[2,384,768]{2,1,0:T(8,128)(2,1)S(1)}, bf16[2,384,768]{2,1,0:T(8,128)(2,1)}, u32[]{:S(2)}) copy-start(bf16[2,384,768]{2,1,0:T(8,128)(2,1)} %param.15) | copy-start | bytes 3538948
  316.5 13.1 %copy-start.19 = (f32[768,768]{1,0:T(8,128)S(1)}, f32[768,768]{1,0:T(8,128)}, u32[]{:S(2)}) copy-start(f32[768,768]{1,0:T(8,128)} %copy-done.18) | copy-start | bytes 7077892
  316.6 13.1 %copy-start.23 = (bf16[768,768]{1,0:T(8,128)(2,1)S(1)}, bf16[768,768]{1,0:T(8,128)(2,1)}, u32[]{:S(2)}) copy-start(bf16[768,768]{1,0:T(8,128)(2,1)} %all-reduce.5.cloned.1.call-done) | copy-start | bytes 3538948
  316.6 13.1 %copy-start.40 = (f32[768]{0:T(1024)S(1)}, f32[768]{0:T(1024)}, u32[]{:S(2)}) copy-start(f32[768]{0:T(1024)} %param.29) | copy-start | bytes 9220
  (33 other events, 67.3 us)
Sparse Core Ops, SparseCore 0:
  55.8 56.7 all-reduce.4
  134.3 55.4 all-reduce.6
  198.0 55.4 all-reduce.8
  256.3 57.4 all-reduce.10
Sparse Core Ops, SparseCore 1:
  57.7 23.4 all-gather.4
  82.6 22.7 all-gather.2
